TPU v7x, 256 devices: a whole 4x4x8 slice. The times are simulated.
256 devices in a mesh: band: 64 (over z_lo, x, y, core), chan: 4 (over z_hi).
Axes of the slice: x: 4, y: 4, z: 8 (z_hi: 4, z_lo: 2; z = z_hi * 2 + z_lo), core: 2. Of those that a mesh axis runs over, the one named last changes fastest.
Arguments:
- video: bfloat16 [3, 2, 512, 512], P(None, None, 'band'), may hold values from -6 to 6
- weight_one: bfloat16 [27, 12, 128], P(None, None, 'chan'), may hold values from -0.3125 to 0.3125
- weight_two: bfloat16 [27, 512, 256], P(None, 'chan'), may hold values from -0.0546875 to 0.0546875
- cotangent: bfloat16 [256, 2, 128, 128], P('chan', None, 'band'), may hold values from -6 to 6
Outputs:
- latent: bfloat16 [256, 2, 128, 128], P('chan', None, 'band')
- grad_one: float32 [27, 12, 128], P(None, None, 'chan')
- grad_two: float32 [27, 512, 256], P(None, 'chan')
All inputs are finite; a program needn't handle non-finite values.
Results may differ from a plain program's by a relative error of at most 0.015.
Values may be sent and summed in bfloat16 or wider, within the bound.
No kernel may reach another device: no remote copies, remote signals or barrier semaphores. Data moves between devices by JAX's collectives and lax.ppermute only.
A program may use at most 64 MiB of HBM per device.

v0:
```python
import math

import jax
import jax.numpy as jnp
from jax import lax
from jax.experimental import pallas as pl
from jax.experimental.pallas import tpu as pltpu
from jax.sharding import PartitionSpec as P

BF = jnp.bfloat16
F32 = jnp.float32


def iota(shape, axis):
    return lax.broadcasted_iota(jnp.int32, shape, axis)


def matrix_kernel(col_ref, row_ref, sel_ref):
    u, w = iota((512, 128), 0), iota((512, 128), 1)
    for s in range(2):
        hit = ((u >> 2) == w) & (((u >> 1) & 1) == s)
        for t in range(2):
            value = 0.5 if t == 0 else jnp.where((u & 1) == 1, -0.5, 0.5)
            at = (s * 2 + t) * 128
            col_ref[:, at : at + 128] = jnp.where(hit, value, 0.0).astype(BF)
    at, lane = iota((256, 128), 0), iota((256, 128), 1)
    m, r, f, tb = at & 15, (at >> 4) & 3, (at >> 6) & 1, at >> 7
    wi = (m * 11) >> 5
    y = 4 * r + 2 * wi + tb + 2
    for part in range(3):
        hit = (lane == (m - 3 * wi) * 16 + f * 8 + y - 8 * part) & (m < 12)
        hit = hit & (y >= 8 * part) & (y < 8 * part + 8)
        row_ref[part] = jnp.where(hit, 1.0, 0.0).astype(BF)
    at, lane = iota((128, 256), 0), iota((128, 256), 1)
    c = (at * 57) >> 9
    tap = at - 9 * c
    b = (tap * 11) >> 5
    e = tap - 3 * b
    target = ((c >> 1) & 1) * 128 + (e * 2 + (c & 1)) * 16 + b * 3 + (c >> 2)
    for p in range(4):
        hit = (lane == target + (p & 1) * 32 + (p >> 1) * 3) & (at < 108)
        sel_ref[p] = jnp.where(hit, 1.0, 0.0).astype(BF)


def dot(a, b, ca=1, cb=0):
    return lax.dot_general(a, b, (((ca,), (cb,)), ((), ())), preferred_element_type=F32)


def edges_kernel(video_ref, own_ref, inner_ref, outer_ref, video_out, own_out, rows):
    core = lax.axis_index("band") % 2
    video_out[...] = video_ref[...]
    own_out[...] = own_ref[...]
    rows[...] = own_ref[...].astype(F32)
    for ref, r in ((inner_ref, 1 - core), (outer_ref, core)):
        ref[:48, :] = video_ref[...]
        edge = rows[pl.ds(r, 128, stride=2), :].astype(BF)
        for i in range(4):
            ref[48:, i * 128 : i * 128 + 128] = edge[i * 32 : i * 32 + 32, :]


def grown_kernel(own_ref, inner_ref, outer_ref, _, __, out_ref):
    core = lax.axis_index("band") % 2
    out_ref[:256, :] = own_ref[...]
    for side, ref in ((1 - core, inner_ref), (core, outer_ref)):
        for i in range(4):
            at = pl.multiple_of(256 + side * 128 + i * 32, 32)
            out_ref[pl.ds(at, 32), :] = ref[48:, i * 128 : i * 128 + 128]


def shifted(x, step):
    lanes = x.shape[1]
    lane = lax.broadcasted_iota(jnp.int32, x.shape, 1) % 128
    if step == -1:
        return jnp.where(lane == 0, 0.0, pltpu.roll(x, 1, 1))
    return jnp.where(lane == 127, 0.0, pltpu.roll(x, lanes - 1, 1))


def forward_kernel(
    inner_ref, own_ref, outer_ref, col_ref, row_ref, sel_ref, w1_ref, cot_ref,
    xc_ref, pre_ref, win_ref, cot_out, one, two,
):
    band = lax.axis_index("band")
    core = band % 2
    cot_out[...] = cot_ref[...]
    last = lax.axis_size("band") - 1
    v = (
        dot(row_ref[2 - 2 * core][:, :48], inner_ref[:48, :])
        + dot(row_ref[1, :, :48], own_ref[...])
        + dot(row_ref[2 * core][:, :48], outer_ref[:48, :])
    ).astype(BF)
    h = dot(v, col_ref[...])
    top, low = h[:128], h[128:]
    for pm, half in enumerate((top + low, top - low)):
        even, odd = half[:, :256], half[:, 256:]
        streams = (shifted(odd, -1), even, odd, shifted(even, 1))
        for st in range(8):
            part = streams[st // 2][:, (st % 2) * 128 : (st % 2) * 128 + 128].astype(BF)
            for f in range(2):
                for r in range(4):
                    at = (f * 4 + r) * 16
                    one[f, pm * 128 + st * 16 : pm * 128 + st * 16 + 16, r * 128 : r * 128 + 128] = part[
                        at : at + 16, :
                    ]
    w1a, w1b = (
        jnp.concatenate([dot(w1_ref[a], sel_ref[p], 0, 0) for p in range(4)], 0).astype(BF)
        for a in range(2)
    )
    pres = (dot(w1b, one[0]), dot(w1a, one[0]) + dot(w1b, one[1]))
    lane = lax.broadcasted_iota(jnp.int32, (32, 512), 1)
    keep = ((lane >= 128) | (band > 0)) & ((lane < 384) | (band < last))
    for f in range(2):
        pre = pres[f]
        pre_ref[:, f * 256 : f * 256 + 256] = pre[:, 128:384]
        win_ref[:, f * 256 : f * 256 + 256] = one[f, :, 128:384]
        act = pre * jax.nn.sigmoid(pre)
        p, q, r, s = act[:32], act[32:64], act[64:96], act[96:]
        pq, pmq, rs, rms = p + q, p - q, r + s, r - s
        parts = (pq + rs, pmq + rms, pq - rs, pmq - rms)
        for k in range(4):
            part = jnp.where(keep, parts[k] * 0.5, 0.0)
            for r in range(4):
                two[r, pl.ds(k, 32, stride=4), :] = part[:, r * 128 : r * 128 + 128]
        x = jnp.concatenate([two[r] for r in range(4)], 1)
        for e, xe in enumerate((shifted(x, -1), x, shifted(x, 1))):
            xe = xe.astype(BF)
            for b in range(3):
                at = (b * 3 + e) * 128
                xc_ref[at : at + 128, f * 256 : f * 256 + 256] = xe[:, b * 128 : b * 128 + 256]


def hold_kernel(_, __, ___):
    pass


def latent_kernel(xc_ref, w2_ref, keep_ref, send_ref, lat):
    out = dot(w2_ref[2304:, :], xc_ref[...], 0, 0)
    more = dot(w2_ref[1152:2304, :], xc_ref[:, :256], 0, 0)
    lat[:, :256] = out[:, :256].astype(BF)
    lat[:, 256:] = (out[:, 256:] + more).astype(BF)
    chan = lax.axis_index("chan")
    for ref, i, k in ((keep_ref, 0, 0), (send_ref, 0, 1), (send_ref, 1, 2), (keep_ref, 1, 3)):
        ref[i] = lat[pl.ds(pl.multiple_of((chan ^ k) * 64, 64), 64), :]


def second_grad_kernel(
    xc_ref, c0_ref, c1_ref, c2_ref, c3_ref, lkeep_ref, lgot_ref,
    grown, keep_ref, send_ref, lown_ref, lsend_ref, rows, *, scale
):
    lown_ref[...] = lkeep_ref[0].astype(F32) + lgot_ref[0].astype(F32)
    lsend_ref[...] = (lkeep_ref[1].astype(F32) + lgot_ref[1].astype(F32)).astype(BF)
    chan = lax.axis_index("chan")
    core = lax.axis_index("band") % 2
    for k, ref in enumerate((c0_ref, c1_ref, c2_ref, c3_ref)):
        rows[...] = ref[...].astype(F32)
        at = pl.multiple_of((chan ^ k) * 64, 64)
        for f in range(2):
            for r in range(2):
                lane = f * 512 + r * 128 + 128
                part = rows[pl.ds(f * 2 + r, 64, stride=4), :]
                grown[pl.ds(at, 64), lane : lane + 128] = part.astype(BF)
            for side in range(2):
                lane = f * 512 + side * 384
                part = rows[pl.ds(256 + side * 128 + f, 64, stride=2), :]
                grown[pl.ds(at, 64), lane : lane + 128] = part.astype(BF)

    def put(early_ref, late_ref):
        c1 = grown[:, 640:896]
        early = dot(xc_ref[:, :256], c1, 1, 1) * scale
        late = (dot(xc_ref[:, :256], grown[:, 128:384], 1, 1) + dot(xc_ref[:, 256:], c1, 1, 1)) * scale
        for ref, g in ((early_ref, early), (late_ref, late)):
            ref[:1152, :] = g[:, :128].astype(BF)
            ref[1152:, :] = g[:, 128:].astype(BF)

    @pl.when(core == 0)
    def _():
        put(keep_ref, send_ref)

    @pl.when(core == 1)
    def _():
        put(send_ref, keep_ref)


def backward_kernel(grown, pre_ref, win_ref, w2_ref, sel_ref, g1_ref, back_s, *, scale):
    z0 = z1 = 0.0
    for b in range(3):
        lo = (2 - b) * 128
        c0, c1 = grown[:, lo : lo + 256], grown[:, 512 + lo : 768 + lo]
        wa = w2_ref[1152 + b * 384 : 1536 + b * 384, :]
        wb = w2_ref[2304 + b * 384 : 2688 + b * 384, :]
        z0 = z0 + dot(wb, c0) + dot(wa, c1)
        z1 = z1 + dot(wb, c1)
    for f, z in enumerate((z0, z1)):
        z = z[128:256] + shifted(z[:128], 1) + shifted(z[256:], -1)
        back_s[0], back_s[1] = z[:, :128], z[:, 128:]
        a0, a1, a2, a3 = (
            jnp.concatenate([back_s[r, pl.ds(k, 32, stride=4), :] for r in range(2)], 1)
            for k in range(4)
        )
        s01, d01, s23, d23 = a0 + a1, a0 - a1, a2 + a3, a2 - a3
        act = jnp.concatenate([s01 + s23, d01 + d23, s01 - s23, d01 - d23], 0) * 0.5
        pre = pre_ref[:, f * 256 : f * 256 + 256]
        gate = jax.nn.sigmoid(pre)
        back = (act * gate * (1.0 + pre * (1.0 - gate))).astype(BF)
        if f == 0:
            late = dot(back, win_ref[:, :256], 1, 1)
        else:
            early = dot(back, win_ref[:, :256], 1, 1)
            late = late + dot(back, win_ref[:, 256:], 1, 1)
    for a, g in enumerate((early, late)):
        g = g * scale
        hi = g.astype(BF)
        lo = (g - hi.astype(F32)).astype(BF)
        total = 0.0
        for p in range(4):
            rows = slice(32 * p, 32 * p + 32)
            total = total + dot(hi[rows], sel_ref[p], 1, 1)
            total = total + dot(lo[rows], sel_ref[p], 1, 1)
        g1_ref[32 * a : 32 * a + 32, :] = total.astype(BF)


def join_kernel(keep_ref, got_ref, g1_ref, sum_ref):
    sum_ref[:2304, :] = (keep_ref[...].astype(F32) + got_ref[...].astype(F32)).astype(BF)
    sum_ref[2304:, :] = g1_ref[...]


def share_kernel(got_ref, lown_ref, lgot_ref, out_ref, lat_ref, rows, wide, *, count):
    lat = lown_ref[...] + lgot_ref[...].astype(F32)
    for i in range(4):
        rows[pl.ds(i, 64, stride=4), :] = lat[:, i * 128 : i * 128 + 128]
    lat_ref[...] = rows[...].astype(BF)
    size = got_ref.shape[0] // count
    bunch = 8 if count % 8 == 0 else count
    block = bunch * size
    total = got_ref[:block, :].astype(F32)
    for i in range(block, count * size, block):
        total = total + got_ref[i : i + block, :].astype(F32)
    wide[...] = total
    total = wide[:size, :]
    for i in range(1, bunch):
        total = total + wide[i * size : i * size + size, :]
    for i in range(bunch):
        wide[i * size : i * size + size, :] = total
    total = wide[...].astype(BF)
    for i in range(0, count * size, block):
        out_ref[i : i + block, :] = total


def widen(from_ref, wide, to_ref, sems, first):
    copies = []
    for i in range(3):
        at = i * 384
        wide[at : at + 384, :128] = from_ref[at : at + 384, :].astype(F32)
        wide[at : at + 384, 128:] = from_ref[1152 + at : 1536 + at, :].astype(F32)
        rows = pl.ds(at, 384)
        copies.append(pltpu.make_async_copy(wide.at[rows], to_ref.at[rows], sems.at[first + i]))
        copies[-1].start()
    return copies


def first_half_kernel(mine_ref, g2_ref, g1_ref, zero, own, sems):
    core = lax.axis_index("band") % 2
    zero[...] = jnp.zeros((1152, 256), F32)
    clear = pltpu.make_async_copy(zero, g2_ref.at[0], sems.at[0])
    clear.start()
    copies = [clear] + widen(mine_ref, own, g2_ref.at[1 + core], sems, 1)
    g1_ref[...] = mine_ref[2304:, :]
    for copy in copies:
        copy.wait()


def other_half_kernel(_, mine_ref, other_ref, g2_ref, g1_ref, half, taps_s, sems):
    core = lax.axis_index("band") % 2
    both = mine_ref[...].astype(F32) + other_ref[2304:2368, :].astype(F32)
    taps_s[...] = jnp.zeros((12, 27, 32), F32)
    for a in range(2):
        taps = jnp.transpose(both[32 * a : 32 * a + 32, :])
        for c in range(12):
            taps_s[c, 9 * a + 9 : 9 * a + 18, :] = taps[9 * c : 9 * c + 9, :]
    first = pltpu.make_async_copy(taps_s, g1_ref, sems.at[3])
    first.start()
    for copy in [first] + widen(other_ref, half, g2_ref.at[2 - core], sems, 0):
        copy.wait()


VMEM, HBM = pltpu.VMEM, pltpu.HBM


def call(kernel, outs, scratch, flops, *args, far=(), far_out=(), aliases=None):
    return pl.pallas_call(
        kernel,
        out_shape=[jax.ShapeDtypeStruct(*o) for o in outs],
        in_specs=[pl.BlockSpec(memory_space=HBM if i in far else VMEM) for i in range(len(args))],
        out_specs=[pl.BlockSpec(memory_space=HBM if i in far_out else VMEM) for i in range(len(outs))],
        scratch_shapes=[s if not isinstance(s, tuple) else pltpu.VMEM(*s) for s in scratch],
        input_output_aliases=aliases or {},
        compiler_params=pltpu.CompilerParams(vmem_limit_bytes=20 * 1024 * 1024),
        cost_estimate=pl.CostEstimate(flops=flops, bytes_accessed=1 << 20, transcendentals=0),
    )(*args)


def on_device(video, weight_one, weight_two, cotangent):
    n = lax.axis_size("band")
    flip = [(i, i ^ 1) for i in range(n)]
    frames, half_rows, half_cols = video.shape[1], n * 4, video.shape[3] // 2
    scale_one = 1.0 / math.sqrt(frames * half_rows * half_cols)
    scale_two = 1.0 / math.sqrt(frames * (half_rows // 2) * (half_cols // 2))

    flat, own = video.reshape(48, 512), cotangent.reshape(256, 128)

    def swap(x, k):
        return lax.ppermute(x, "chan", [(i, i ^ k) for i in range(4)])

    inner, outer, flat, own = call(
        edges_kernel,
        [((80, 512), BF), ((80, 512), BF), ((48, 512), BF), ((256, 128), BF)],
        [((256, 128), F32)],
        1 << 20,
        flat, own,
    )
    inner = lax.ppermute(inner, "band", flip)
    outer = lax.ppermute(outer, "band", [(i, i + 1 - 2 * (i % 2 == 0)) for i in range(1, n - 1)])
    cols, rows, sel = call(
        matrix_kernel,
        [((512, 512), BF), ((3, 256, 128), BF), ((4, 128, 256), BF)],
        [],
        1 << 20,
    )
    w1 = weight_one[9:].reshape(2, 9, 12, 32).transpose(0, 2, 1, 3).reshape(2, 108, 32)
    w1 = jnp.pad(w1, ((0, 0), (0, 20), (0, 0)))
    (own,) = call(
        grown_kernel, [((512, 128), BF)], [], 1 << 20, own, inner, outer, sel, w1,
        far=(3, 4),
    )
    near = swap(own, 1)
    w2 = weight_two.reshape(3456, 256)
    xc, pre, win, own = call(
        forward_kernel,
        [((1152, 512), BF), ((128, 512), F32), ((256, 512), BF), ((512, 128), BF)],
        [((2, 256, 512), BF), ((4, 128, 128), F32)],
        1 << 30,
        inner, flat, outer, cols, rows, sel, w1, own,
    )
    far = swap(own, 3)
    (near,) = call(
        hold_kernel, [((512, 128), BF)], [], 1 << 10, near, xc, far=(0, 1), far_out=(0,), aliases={0: 0}
    )
    others = [near, swap(near, 3), far]
    lat_keep, lat_send = call(
        latent_kernel, [((2, 64, 512), BF)] * 2, [((256, 512), BF)], 1 << 30, xc, w2
    )
    lat_got = swap(lat_send, 1)

    def second_grad(*refs):
        second_grad_kernel(*refs, scale=scale_two)

    cot, keep, send, lat_own, lat_send = call(
        second_grad,
        [
            ((256, 1024), BF), ((2304, 128), BF), ((2304, 128), BF),
            ((64, 512), F32), ((64, 512), BF),
        ],
        [((512, 128), F32)],
        1 << 30,
        xc, own, *others, lat_keep, lat_got,
    )
    lat_got = swap(lat_send, 3)
    got = lax.ppermute(send, "band", flip)

    def backward(*refs):
        backward_kernel(*refs, scale=scale_one)

    (g1,) = call(
        backward, [((64, 128), BF)], [((2, 128, 128), F32)], 1 << 30, cot, pre, win, w2, sel
    )
    (part,) = call(join_kernel, [((2368, 128), BF)], [], 1 << 20, keep, got, g1)
    half = n // 2
    groups = [[2 * i + c for i in range(half)] for c in range(2)]

    def exchange(x):
        x = x.reshape(half, 1184 // half, 2, 128)
        x = lax.all_to_all(x, "band", 0, 0, tiled=True, axis_index_groups=groups)
        return x.reshape(2368, 128)

    def share(*refs):
        share_kernel(*refs, count=half)

    part = exchange(part)
    mine, latent = call(
        share,
        [((2368, 128), BF), ((256, 128), BF)],
        [((256, 128), F32), ((2368 // half * min(half, 8), 128), F32)],
        1 << 20,
        part, lat_own, lat_got,
    )
    mine = exchange(mine)
    other = lax.ppermute(mine, "band", flip)
    g2, g1 = call(
        first_half_kernel,
        [((3, 1152, 256), F32), ((64, 128), BF)],
        [((1152, 256), F32), ((1152, 256), F32), pltpu.SemaphoreType.DMA((4,))],
        1 << 20,
        mine,
        far_out=(0,),
    )
    g2, g1 = call(
        other_half_kernel,
        [((3, 1152, 256), F32), ((12, 27, 32), F32)],
        [((1152, 256), F32), ((12, 27, 32), F32), pltpu.SemaphoreType.DMA((4,))],
        1 << 20,
        g2, g1, other,
        far=(0,), far_out=(0, 1), aliases={0: 0},
    )
    return latent.reshape(64, 2, 2, 128), jnp.transpose(g1, (1, 0, 2)), g2.reshape(27, 128, 256)


def solution(mesh):
    return jax.shard_map(
        on_device,
        mesh=mesh,
        in_specs=(
            P(None, None, "band", None),
            P(None, None, "chan"),
            P(None, "chan", None),
            P("chan", None, "band", None),
        ),
        out_specs=(P("chan", None, "band", None), P(None, None, "chan"), P(None, "chan", None)),
        check_vma=False,
    )
```

profile of v0, /device:TPU:1, one launch (start us, length us, event | category | flops | bytes accessed | tf_op | source)
XLA Modules:
  0.0 78.2 jit_solution(16681047860302810828)
XLA Ops:
  0.6 0.8 %copy-done = bf16[64,2,2,128]{3,2,1,0:T(2,128)(2,1)S(1)} copy-done((bf16[64,2,2,128]{3,2,1,0:T(2,128)(2,1)S(1)}, bf16[64,2,2,128]{3,2,1,0:T(2,128)(2,1)}, u32[]{:S(2)}) %copy-start) | copy-done | bytes 65560
  1.5 0.8 %copy-done.1 = bf16[3,2,8,512]{3,2,1,0:T(8,128)(2,1)S(1)} copy-done((bf16[3,2,8,512]{3,2,1,0:T(8,128)(2,1)S(1)}, bf16[3,2,8,512]{3,2,1,0:T(8,128)(2,1)}, u32[]{:S(2)}) %copy-start.1) | copy-done | bytes 49176
  2.3 3.3 %collective-permute-start = (bf16[80,512]{1,0:T(8,128)(2,1)S(1)}, bf16[80,512]{1,0:T(8,128)(2,1)S(1)}, u32[]{:S(2)}, u32[]{:S(2)}) collective-permute-start(bf16[80,512]{1,0:T(8,128)(2,1)S(1)} %get-tuple-element.27), channel_id=1, source_target_pairs={{0,4},{4,0},{8,12},{12,8},{16,20},{20,16},{24,28},{28,24},{32,36},... | collective-permute-start | bytes 245768 | tf_op jit(solution)/shard_map/ppermute | solution.py:320
  5.6 1.9 %collective-permute-start.1 = (bf16[80,512]{1,0:T(8,128)(2,1)S(1)}, bf16[80,512]{1,0:T(8,128)(2,1)S(1)}, u32[]{:S(2)}, u32[]{:S(2)}) collective-permute-start(bf16[80,512]{1,0:T(8,128)(2,1)S(1)} %get-tuple-element.29), channel_id=1, source_target_pairs={{4,8},{8,4},{12,16},{16,12},{20,24},{24,20},{28,32},{32,28},{36,40... | collective-permute-start | bytes 245768 | tf_op jit(solution)/shard_map/ppermute | solution.py:321
  7.6 0.9 %slice.3 = bf16[18,12,32]{2,0,1:T(8,128)(2,1)S(1)} slice(bf16[27,12,32]{2,0,1:T(8,128)(2,1)} %param.5), slice={[9:27], [0:12], [0:32]} | slice | bytes 27648 | tf_op jit(solution)/shard_map/slice | solution.py:328
  8.6 0.5 shard_map.68
  9.1 0.0 collective-permute-done.inner_ref
  9.1 2.3 %collective-permute-done.1.outer_ref = bf16[80,512]{1,0:T(8,128)(2,1)S(1)} collective-permute-done((bf16[80,512]{1,0:T(8,128)(2,1)S(1)}, bf16[80,512]{1,0:T(8,128)(2,1)S(1)}, u32[]{:S(2)}, u32[]{:S(2)}) %collective-permute-start.1) | collective-permute-done | bytes 81952 | tf_op jit(solution)/shard_map/ppermute | solution.py:321
  11.4 1.3 %collective-permute-start.2 = (bf16[512,128]{1,0:T(8,128)(2,1)S(1)}, bf16[512,128]{1,0:T(8,128)(2,1)S(1)}, u32[]{:S(2)}, u32[]{:S(2)}) collective-permute-start(bf16[512,128]{1,0:T(8,128)(2,1)S(1)} %shard_map.69.cot_ref), channel_id=1, source_target_pairs={{0,1},{1,0},{2,3},{3,2},{4,5},{5,4},{6,7},{7,6},{8,9},{9,8},{10,11... | collective-permute-start | bytes 393224 | tf_op jit(solution)/shard_map/ppermute | solution.py:311
  12.8 1.2 %shard_map.70 = (bf16[1152,512]{1,0:T(8,128)(2,1)S(1)}, f32[128,512]{1,0:T(8,128)S(1)}, bf16[256,512]{1,0:T(8,128)(2,1)S(1)}, bf16[512,128]{1,0:T(8,128)(2,1)S(1)}) custom-call(bf16[80,512]{1,0:T(8,128)(2,1)S(1)} %collective-permute-done.inner_ref, bf16[48,512]{1,0:T(8,128)(2,1)S(1)} %get-tuple-element.28.own_ref, ...), custom_call_target="tpu_custom_call" | custom-call | flops 1073741824 | bytes 1048576 | tf_op jit(solution)/shard_map/pallas_call | solution.py:289
  13.9 4.3 %collective-permute-start.4 = (bf16[512,128]{1,0:T(8,128)(2,1)S(1)}, bf16[512,128]{1,0:T(8,128)(2,1)S(1)}, u32[]{:S(2)}, u32[]{:S(2)}) collective-permute-start(bf16[512,128]{1,0:T(8,128)(2,1)S(1)} %get-tuple-element.35.refs_1_), channel_id=1, source_target_pairs={{0,3},{1,2},{2,1},{3,0},{4,7},{5,6},{6,5},{7,4},{8,11},{9,10},{10,... | collective-permute-start | bytes 393224 | tf_op jit(solution)/shard_map/ppermute | solution.py:311
  18.2 0.7 shard_map.72
  19.0 1.3 %collective-permute-start.5 = (bf16[2,64,512]{2,1,0:T(8,128)(2,1)S(1)}, bf16[2,64,512]{2,1,0:T(8,128)(2,1)S(1)}, u32[]{:S(2)}, u32[]{:S(2)}) collective-permute-start(bf16[2,64,512]{2,1,0:T(8,128)(2,1)S(1)} %get-tuple-element.37), channel_id=1, source_target_pairs={{0,1},{1,0},{2,3},{3,2},{4,5},{5,4},{6,7},{7,6},{8,9},{9,8},{10,11... | collective-permute-start | bytes 393224 | tf_op jit(solution)/shard_map/ppermute | solution.py:311
  20.3 1.3 %collective-permute-start.3 = (bf16[512,128]{1,0:T(8,128)(2,1)S(1)}, bf16[512,128]{1,0:T(8,128)(2,1)S(1)}, u32[]{:S(2)}, u32[]{:S(2)}) collective-permute-start(bf16[512,128]{1,0:T(8,128)(2,1)S(1)} %shard_map.71.refs_2_), channel_id=1, source_target_pairs={{0,3},{1,2},{2,1},{3,0},{4,7},{5,6},{6,5},{7,4},{8,11},{9,10},{10,... | collective-permute-start | bytes 393224 | tf_op jit(solution)/shard_map/ppermute | solution.py:311
  21.6 0.6 collective-permute-done.4.refs_4_
  22.2 3.4 %collective-permute-done.5.refs_6_ = bf16[2,64,512]{2,1,0:T(8,128)(2,1)S(1)} collective-permute-done((bf16[2,64,512]{2,1,0:T(8,128)(2,1)S(1)}, bf16[2,64,512]{2,1,0:T(8,128)(2,1)S(1)}, u32[]{:S(2)}, u32[]{:S(2)}) %collective-permute-start.5) | collective-permute-done | bytes 131104 | tf_op jit(solution)/shard_map/ppermute | solution.py:311
  25.5 4.7 %collective-permute-done.3.refs_3_ = bf16[512,128]{1,0:T(8,128)(2,1)S(1)} collective-permute-done((bf16[512,128]{1,0:T(8,128)(2,1)S(1)}, bf16[512,128]{1,0:T(8,128)(2,1)S(1)}, u32[]{:S(2)}, u32[]{:S(2)}) %collective-permute-start.3) | collective-permute-done | bytes 131104 | tf_op jit(solution)/shard_map/ppermute | solution.py:311
  30.2 0.9 %shard_map.73 = (bf16[256,1024]{1,0:T(8,128)(2,1)S(1)}, bf16[2304,128]{1,0:T(8,128)(2,1)S(1)}, bf16[2304,128]{1,0:T(8,128)(2,1)S(1)}, f32[64,512]{1,0:T(8,128)S(1)}, bf16[64,512]{1,0:T(8,128)(2,1)S(1)}) custom-call(bf16[1152,512]{1,0:T(8,128)(2,1)S(1)} %get-tuple-element.34.__.xc_ref.refs_0_, bf16[512,128]{1,0:T(8,128)(2,1)S(1)} %get-tuple-element.35.refs_1_, ...), custom_call_target="tpu_custom_call" | custom-call | flops 1073741824 | bytes 1048576 | tf_op jit(solution)/shard_map/pallas_call | solution.py:289
  31.1 0.1 collective-permute-start.6
  31.2 1.4 %shard_map.74.g1_ref = bf16[64,128]{1,0:T(8,128)(2,1)S(1)} custom-call(bf16[256,1024]{1,0:T(8,128)(2,1)S(1)} %get-tuple-element.40.refs_0_, f32[128,512]{1,0:T(8,128)S(1)} %get-tuple-element.41.refs_1_, bf16[256,512]{1,0:T(8,128)(2,1)S(1)} %get-tuple-element.42.refs_2_, bf16[3456,256]{1,0:T(8,128)(2,1)S(1)} %bitcast.21, ...), custom_call_target="tpu_custom_call" | custom-call | flops 1073741824 | bytes 1048576 | tf_op jit(solution)/shard_map/pallas_call | solution.py:289
  32.6 0.6 collective-permute-done.6.got_ref
  33.2 1.0 %shard_map.75 = bf16[2368,128]{1,0:T(8,128)(2,1)} custom-call(bf16[2304,128]{1,0:T(8,128)(2,1)S(1)} %get-tuple-element.38.keep_ref, bf16[2304,128]{1,0:T(8,128)(2,1)S(1)} %collective-permute-done.6.got_ref, bf16[64,128]{1,0:T(8,128)(2,1)S(1)} %shard_map.74.g1_ref), custom_call_target="tpu_custom_call" | custom-call | flops 1048576 | bytes 1048576 | tf_op jit(solution)/shard_map/pallas_call | solution.py:289
  34.2 11.2 %all-to-all-start = ((bf16[32,37,2,128]{3,2,1,0:T(2,128)(2,1)}), bf16[32,37,2,128]{3,2,1,0:T(2,128)(2,1)S(1)}, u32[]{:S(2)}, u32[]{:S(2)}) async-start(bf16[32,37,2,128]{3,2,1,0:T(2,128)(2,1)} %bitcast.6), calls=%async_computation | async-start | bytes 1212416 | tf_op jit(solution)/shard_map/all_to_all | solution.py:381
  45.4 1.5 %collective-permute-start.7 = (bf16[64,512]{1,0:T(8,128)(2,1)S(1)}, bf16[64,512]{1,0:T(8,128)(2,1)S(1)}, u32[]{:S(2)}, u32[]{:S(2)}) collective-permute-start(bf16[64,512]{1,0:T(8,128)(2,1)S(1)} %get-tuple-element.44), channel_id=1, source_target_pairs={{0,3},{1,2},{2,1},{3,0},{4,7},{5,6},{6,5},{7,4},{8,11},{9,10},{10,... | collective-permute-start | bytes 196616 | tf_op jit(solution)/shard_map/ppermute | solution.py:311
  46.9 8.2 %collective-permute-done.7.refs_2_ = bf16[64,512]{1,0:T(8,128)(2,1)S(1)} collective-permute-done((bf16[64,512]{1,0:T(8,128)(2,1)S(1)}, bf16[64,512]{1,0:T(8,128)(2,1)S(1)}, u32[]{:S(2)}, u32[]{:S(2)}) %collective-permute-start.7) | collective-permute-done | bytes 65568 | tf_op jit(solution)/shard_map/ppermute | solution.py:311
  55.1 1.0 %all-to-all-done = bf16[32,37,2,128]{3,2,1,0:T(2,128)(2,1)S(1)} async-done(((bf16[32,37,2,128]{3,2,1,0:T(2,128)(2,1)}), bf16[32,37,2,128]{3,2,1,0:T(2,128)(2,1)S(1)}, u32[]{:S(2)}, u32[]{:S(2)}) %all-to-all-start) | async-done | bytes 606240 | tf_op jit(solution)/shard_map/all_to_all | solution.py:381
  56.2 0.7 shard_map.76
  56.8 14.9 %all_to_all.10 = bf16[32,37,2,128]{3,2,1,0:T(2,128)(2,1)S(1)} all-to-all(bf16[32,37,2,128]{3,2,1,0:T(2,128)(2,1)S(1)} %bitcast.17), channel_id=1, replica_groups={{0,8,16,24,32,40,48,56,64,72,80,88,96,104,112,120,128,136,144,152,160,1..., dimensions={0} | all-to-all | bytes 1212416 | tf_op jit(solution)/shard_map/all_to_all | solution.py:381
  71.7 3.6 %collective-permute-start.8 = (bf16[2368,128]{1,0:T(8,128)(2,1)S(1)}, bf16[2368,128]{1,0:T(8,128)(2,1)S(1)}, u32[]{:S(2)}, u32[]{:S(2)}) collective-permute-start(bf16[2368,128]{1,0:T(8,128)(2,1)S(1)} %bitcast.15), channel_id=1, source_target_pairs={{0,4},{4,0},{8,12},{12,8},{16,20},{20,16},{24,28},{28,24},{32,36},... | collective-permute-start | bytes 1818632 | tf_op jit(solution)/shard_map/ppermute | solution.py:396
  75.3 1.5 %shard_map.77 = (f32[3,1152,256]{2,1,0:T(8,128)}, bf16[64,128]{1,0:T(8,128)(2,1)S(1)}) custom-call(bf16[2368,128]{1,0:T(8,128)(2,1)S(1)} %bitcast.16), custom_call_target="tpu_custom_call" | custom-call | flops 1048576 | bytes 1048576 | tf_op jit(solution)/shard_map/pallas_call | solution.py:289
  76.9 0.1 collective-permute-done.8.other_ref
  77.0 1.2 %shard_map.78 = (f32[3,1152,256]{2,1,0:T(8,128)}, f32[12,27,32]{2,1,0:T(8,128)}) custom-call(f32[3,1152,256]{2,1,0:T(8,128)} %get-tuple-element.47._, bf16[64,128]{1,0:T(8,128)(2,1)S(1)} %get-tuple-element.48.mine_ref, bf16[2368,128]{1,0:T(8,128)(2,1)S(1)} %collective-permute-done.8.other_ref), custom_call_target="tpu_custom_call", output_to_operand_aliasing={{0}: (0, {})} | custom-call | flops 1048576 | bytes 1048576 | tf_op jit(solution)/shard_map/pallas_call | solution.py:289
  (12 shorter events, 0.2 us)
Async XLA Ops:
  0.6 0.8 %copy-start = (bf16[64,2,2,128]{3,2,1,0:T(2,128)(2,1)S(1)}, bf16[64,2,2,128]{3,2,1,0:T(2,128)(2,1)}, u32[]{:S(2)}) copy-start(bf16[64,2,2,128]{3,2,1,0:T(2,128)(2,1)} %param.7) | copy-start | bytes 196612
  1.5 0.8 %copy-start.1 = (bf16[3,2,8,512]{3,2,1,0:T(8,128)(2,1)S(1)}, bf16[3,2,8,512]{3,2,1,0:T(8,128)(2,1)}, u32[]{:S(2)}) copy-start(bf16[3,2,8,512]{3,2,1,0:T(8,128)(2,1)} %param.4) | copy-start | bytes 147460
  2.3 16.0 %copy-start.2 = (bf16[27,128,256]{2,1,0:T(8,128)(2,1)S(1)}, bf16[27,128,256]{2,1,0:T(8,128)(2,1)}, u32[]{:S(2)}) copy-start(bf16[27,128,256]{2,1,0:T(8,128)(2,1)} %param.6) | copy-start | bytes 5308420
  2.3 6.8 %collective-permute-start = (bf16[80,512]{1,0:T(8,128)(2,1)S(1)}, bf16[80,512]{1,0:T(8,128)(2,1)S(1)}, u32[]{:S(2)}, u32[]{:S(2)}) collective-permute-start(bf16[80,512]{1,0:T(8,128)(2,1)S(1)} %get-tuple-element.27), channel_id=1, source_target_pairs={{0,4},{4,0},{8,12},{12,8},{16,20},{20,16},{24,28},{28,24},{32,36},... | collective-permute-start | bytes 245768 | tf_op jit(solution)/shard_map/ppermute | solution.py:320
  5.6 5.7 %collective-permute-start.1 = (bf16[80,512]{1,0:T(8,128)(2,1)S(1)}, bf16[80,512]{1,0:T(8,128)(2,1)S(1)}, u32[]{:S(2)}, u32[]{:S(2)}) collective-permute-start(bf16[80,512]{1,0:T(8,128)(2,1)S(1)} %get-tuple-element.29), channel_id=1, source_target_pairs={{4,8},{8,4},{12,16},{16,12},{20,24},{24,20},{28,32},{32,28},{36,40... | collective-permute-start | bytes 245768 | tf_op jit(solution)/shard_map/ppermute | solution.py:321
  11.4 8.9 %collective-permute-start.2 = (bf16[512,128]{1,0:T(8,128)(2,1)S(1)}, bf16[512,128]{1,0:T(8,128)(2,1)S(1)}, u32[]{:S(2)}, u32[]{:S(2)}) collective-permute-start(bf16[512,128]{1,0:T(8,128)(2,1)S(1)} %shard_map.69.cot_ref), channel_id=1, source_target_pairs={{0,1},{1,0},{2,3},{3,2},{4,5},{5,4},{6,7},{7,6},{8,9},{9,8},{10,11... | collective-permute-start | bytes 393224 | tf_op jit(solution)/shard_map/ppermute | solution.py:311
  13.9 8.3 %collective-permute-start.4 = (bf16[512,128]{1,0:T(8,128)(2,1)S(1)}, bf16[512,128]{1,0:T(8,128)(2,1)S(1)}, u32[]{:S(2)}, u32[]{:S(2)}) collective-permute-start(bf16[512,128]{1,0:T(8,128)(2,1)S(1)} %get-tuple-element.35.refs_1_), channel_id=1, source_target_pairs={{0,3},{1,2},{2,1},{3,0},{4,7},{5,6},{6,5},{7,4},{8,11},{9,10},{10,... | collective-permute-start | bytes 393224 | tf_op jit(solution)/shard_map/ppermute | solution.py:311
  19.0 6.5 %collective-permute-start.5 = (bf16[2,64,512]{2,1,0:T(8,128)(2,1)S(1)}, bf16[2,64,512]{2,1,0:T(8,128)(2,1)S(1)}, u32[]{:S(2)}, u32[]{:S(2)}) collective-permute-start(bf16[2,64,512]{2,1,0:T(8,128)(2,1)S(1)} %get-tuple-element.37), channel_id=1, source_target_pairs={{0,1},{1,0},{2,3},{3,2},{4,5},{5,4},{6,7},{7,6},{8,9},{9,8},{10,11... | collective-permute-start | bytes 393224 | tf_op jit(solution)/shard_map/ppermute | solution.py:311
  20.3 10.0 %collective-permute-start.3 = (bf16[512,128]{1,0:T(8,128)(2,1)S(1)}, bf16[512,128]{1,0:T(8,128)(2,1)S(1)}, u32[]{:S(2)}, u32[]{:S(2)}) collective-permute-start(bf16[512,128]{1,0:T(8,128)(2,1)S(1)} %shard_map.71.refs_2_), channel_id=1, source_target_pairs={{0,3},{1,2},{2,1},{3,0},{4,7},{5,6},{6,5},{7,4},{8,11},{9,10},{10,... | collective-permute-start | bytes 393224 | tf_op jit(solution)/shard_map/ppermute | solution.py:311
  31.1 2.1 %collective-permute-start.6 = (bf16[2304,128]{1,0:T(8,128)(2,1)S(1)}, bf16[2304,128]{1,0:T(8,128)(2,1)S(1)}, u32[]{:S(2)}, u32[]{:S(2)}) collective-permute-start(bf16[2304,128]{1,0:T(8,128)(2,1)S(1)} %get-tuple-element.39), channel_id=1, source_target_pairs={{0,4},{4,0},{8,12},{12,8},{16,20},{20,16},{24,28},{28,24},{32,36},... | collective-permute-start | bytes 1769480 | tf_op jit(solution)/shard_map/ppermute | solution.py:367
  34.2 22.0 %all-to-all-start = ((bf16[32,37,2,128]{3,2,1,0:T(2,128)(2,1)}), bf16[32,37,2,128]{3,2,1,0:T(2,128)(2,1)S(1)}, u32[]{:S(2)}, u32[]{:S(2)}) async-start(bf16[32,37,2,128]{3,2,1,0:T(2,128)(2,1)} %bitcast.6), calls=%async_computation | async-start | bytes 1212416 | tf_op jit(solution)/shard_map/all_to_all | solution.py:381
  45.4 9.8 %collective-permute-start.7 = (bf16[64,512]{1,0:T(8,128)(2,1)S(1)}, bf16[64,512]{1,0:T(8,128)(2,1)S(1)}, u32[]{:S(2)}, u32[]{:S(2)}) collective-permute-start(bf16[64,512]{1,0:T(8,128)(2,1)S(1)} %get-tuple-element.44), channel_id=1, source_target_pairs={{0,3},{1,2},{2,1},{3,0},{4,7},{5,6},{6,5},{7,4},{8,11},{9,10},{10,... | collective-permute-start | bytes 196616 | tf_op jit(solution)/shard_map/ppermute | solution.py:311
  71.7 5.3 %collective-permute-start.8 = (bf16[2368,128]{1,0:T(8,128)(2,1)S(1)}, bf16[2368,128]{1,0:T(8,128)(2,1)S(1)}, u32[]{:S(2)}, u32[]{:S(2)}) collective-permute-start(bf16[2368,128]{1,0:T(8,128)(2,1)S(1)} %bitcast.15), channel_id=1, source_target_pairs={{0,4},{4,0},{8,12},{12,8},{16,20},{20,16},{24,28},{28,24},{32,36},... | collective-permute-start | bytes 1818632 | tf_op jit(solution)/shard_map/ppermute | solution.py:396
where the time goes:
time: 78.6 us; the launch traced here: 78.2 us
  starting transfers between devices  29.9 us (38%)
  waiting for transfers between devices  20.9 us (27%)
  blocking collectives  14.9 us (19%)
  Pallas kernels  9.08 us (12%)
  local copies, waits for them, and re-layouts  2.63 us (3%)
    ppermute x5, waiting for transfers between devices, swap(): return lax.ppermute(x, 'chan', [(i, i ^ k) for i in range(4)])  16.9 us
    all_to_all x1, blocking collectives, exchange(): x = lax.all_to_all(x, 'band', 0, 0, tiled=True, axis_index_groups=groups)  14.9 us
    all_to_all x1, starting transfers between devices, exchange(): x = lax.all_to_all(x, 'band', 0, 0, tiled=True, axis_index_groups=groups)  11.2 us
    ppermute x5, starting transfers between devices, swap(): return lax.ppermute(x, 'chan', [(i, i ^ k) for i in range(4)])  9.8 us
    pallas_call x12, Pallas kernels, call(): pl.pallas_call(kernel, out_shape=[jax.ShapeDtypeStruct(*o) for o in outs]...  9.08 us
    ppermute x1, starting transfers between devices, on_device(): other = lax.ppermute(mine, 'band', flip)  3.64 us
    ppermute x1, starting transfers between devices, on_device(): inner = lax.ppermute(inner, 'band', flip)  3.33 us
    ppermute x1, waiting for transfers between devices, on_device(): lax.ppermute(outer, 'band', [(i, i + 1 - 2 * (i % 2 == 0)) for i in range...  2.25 us
  transfers between devices with their start and end apart: 10, of which 8 were waited for; matrix products, arithmetic and copies ran while one was open for 1% of the time, Pallas kernels for 7%

commit v1 on v0

--- a/solution.py
+++ b/solution.py
@@ -128,8 +128,12 @@
                 xc_ref[at : at + 128, f * 256 : f * 256 + 256] = xe[:, b * 128 : b * 128 + 256]
 
 
-def hold_kernel(_, __, ___):
-    pass
+def first_rows_kernel(in_ref, _, out_ref):
+    out_ref[...] = in_ref[:256, :]
+
+
+def last_rows_kernel(in_ref, out_ref):
+    out_ref[...] = in_ref[256:, :]
 
 
 def latent_kernel(xc_ref, w2_ref, keep_ref, send_ref, lat):
@@ -143,15 +147,19 @@
 
 
 def second_grad_kernel(
-    xc_ref, c0_ref, c1_ref, c2_ref, c3_ref, lkeep_ref, lgot_ref,
+    xc_ref, c0_ref, c1_ref, c3_ref, own2_ref, outer2_ref, lkeep_ref, lgot_ref,
     grown, keep_ref, send_ref, lown_ref, lsend_ref, rows, *, scale
 ):
     lown_ref[...] = lkeep_ref[0].astype(F32) + lgot_ref[0].astype(F32)
     lsend_ref[...] = (lkeep_ref[1].astype(F32) + lgot_ref[1].astype(F32)).astype(BF)
     chan = lax.axis_index("chan")
     core = lax.axis_index("band") % 2
-    for k, ref in enumerate((c0_ref, c1_ref, c2_ref, c3_ref)):
-        rows[...] = ref[...].astype(F32)
+    for k, ref in enumerate((c0_ref, c1_ref, None, c3_ref)):
+        if ref is None:
+            rows[:256, :] = own2_ref[...].astype(F32)
+            rows[256:, :] = outer2_ref[...].astype(F32)
+        else:
+            rows[...] = ref[...].astype(F32)
         at = pl.multiple_of((chan ^ k) * 64, 64)
         for f in range(2):
             for r in range(2):
@@ -341,10 +349,9 @@
         inner, flat, outer, cols, rows, sel, w1, own,
     )
     far = swap(own, 3)
-    (near,) = call(
-        hold_kernel, [((512, 128), BF)], [], 1 << 10, near, xc, far=(0, 1), far_out=(0,), aliases={0: 0}
-    )
-    others = [near, swap(near, 3), far]
+    (near_part,) = call(first_rows_kernel, [((256, 128), BF)], [], 1 << 10, near, xc, far=(1,))
+    (far_part,) = call(last_rows_kernel, [((256, 128), BF)], [], 1 << 10, far)
+    others = [near, far, swap(near_part, 3), swap(far_part, 1)]
     lat_keep, lat_send = call(
         latent_kernel, [((2, 64, 512), BF)] * 2, [((256, 512), BF)], 1 << 30, xc, w2
     )

time: 78.6 us -> 78.6 us (level)
  waiting for transfers between devices: 20.9 us -> 15.7 us
  starting transfers between devices: 29.9 us -> 35 us
    ppermute x5 -> x6, waiting for transfers between devices: 16.9 us -> 11.9 us  [swap(): return lax.ppermute(x, 'chan', [(i, i ^ k) for i in range(4)])]
    all_to_all x1, starting transfers between devices: 11.2 us -> 14 us  [exchange(): x = lax.all_to_all(x, 'band', 0, 0, tiled=True, axis_index_groups=groups)]
    ppermute x5 -> x6, starting transfers between devices: 9.8 us -> 12.1 us  [swap(): return lax.ppermute(x, 'chan', [(i, i ^ k) for i in range(4)])]
    pallas_call x12 -> x13, Pallas kernels: 9.08 us -> 9.09 us  [call(): pl.pallas_call(kernel, out_shape=[jax.ShapeDtypeStruct(*o) for o in outs]...]
  transfers between devices with their start and end apart: 10 -> 11, of which waited for: 8 -> 8; matrix products, arithmetic and copies ran while one was open for 1% -> 1% of each run, Pallas kernels for 7% -> 7%
where the time goes in v1:
time: 78.6 us; the launch traced here: 78.2 us
  starting transfers between devices  35 us (45%)
  waiting for transfers between devices  15.7 us (20%)
  blocking collectives  15 us (19%)
  Pallas kernels  9.09 us (12%)
  local copies, waits for them, and re-layouts  2.63 us (3%)
    all_to_all x1, blocking collectives, exchange(): x = lax.all_to_all(x, 'band', 0, 0, tiled=True, axis_index_groups=groups)  15 us
    all_to_all x1, starting transfers between devices, exchange(): x = lax.all_to_all(x, 'band', 0, 0, tiled=True, axis_index_groups=groups)  14 us
    ppermute x6, starting transfers between devices, swap(): return lax.ppermute(x, 'chan', [(i, i ^ k) for i in range(4)])  12.1 us
    ppermute x6, waiting for transfers between devices, swap(): return lax.ppermute(x, 'chan', [(i, i ^ k) for i in range(4)])  11.9 us
    pallas_call x13, Pallas kernels, call(): pl.pallas_call(kernel, out_shape=[jax.ShapeDtypeStruct(*o) for o in outs]...  9.09 us
    ppermute x1, starting transfers between devices, on_device(): other = lax.ppermute(mine, 'band', flip)  3.64 us
    ppermute x1, starting transfers between devices, on_device(): inner = lax.ppermute(inner, 'band', flip)  3.33 us
    ppermute x1, waiting for transfers between devices, on_device(): lax.ppermute(outer, 'band', [(i, i + 1 - 2 * (i % 2 == 0)) for i in range...  2.25 us
  transfers between devices with their start and end apart: 11, of which 8 were waited for; matrix products, arithmetic and copies ran while one was open for 1% of the time, Pallas kernels for 7%

profile of v1, /device:TPU:1, one launch (start us, length us, event | category | flops | bytes accessed | tf_op | source)
XLA Modules:
  0.0 78.2 jit_solution(2336105347366613149)
XLA Ops:
  0.6 0.8 %copy-done = bf16[64,2,2,128]{3,2,1,0:T(2,128)(2,1)S(1)} copy-done((bf16[64,2,2,128]{3,2,1,0:T(2,128)(2,1)S(1)}, bf16[64,2,2,128]{3,2,1,0:T(2,128)(2,1)}, u32[]{:S(2)}) %copy-start) | copy-done | bytes 65560
  1.5 0.8 %copy-done.1 = bf16[3,2,8,512]{3,2,1,0:T(8,128)(2,1)S(1)} copy-done((bf16[3,2,8,512]{3,2,1,0:T(8,128)(2,1)S(1)}, bf16[3,2,8,512]{3,2,1,0:T(8,128)(2,1)}, u32[]{:S(2)}) %copy-start.1) | copy-done | bytes 49176
  2.3 3.3 %collective-permute-start = (bf16[80,512]{1,0:T(8,128)(2,1)S(1)}, bf16[80,512]{1,0:T(8,128)(2,1)S(1)}, u32[]{:S(2)}, u32[]{:S(2)}) collective-permute-start(bf16[80,512]{1,0:T(8,128)(2,1)S(1)} %get-tuple-element.27), channel_id=1, source_target_pairs={{0,4},{4,0},{8,12},{12,8},{16,20},{20,16},{24,28},{28,24},{32,36},... | collective-permute-start | bytes 245768 | tf_op jit(solution)/shard_map/ppermute | solution.py:328
  5.6 1.9 %collective-permute-start.1 = (bf16[80,512]{1,0:T(8,128)(2,1)S(1)}, bf16[80,512]{1,0:T(8,128)(2,1)S(1)}, u32[]{:S(2)}, u32[]{:S(2)}) collective-permute-start(bf16[80,512]{1,0:T(8,128)(2,1)S(1)} %get-tuple-element.29), channel_id=1, source_target_pairs={{4,8},{8,4},{12,16},{16,12},{20,24},{24,20},{28,32},{32,28},{36,40... | collective-permute-start | bytes 245768 | tf_op jit(solution)/shard_map/ppermute | solution.py:329
  7.6 0.9 %slice.3 = bf16[18,12,32]{2,0,1:T(8,128)(2,1)S(1)} slice(bf16[27,12,32]{2,0,1:T(8,128)(2,1)} %param.5), slice={[9:27], [0:12], [0:32]} | slice | bytes 27648 | tf_op jit(solution)/shard_map/slice | solution.py:336
  8.6 0.5 shard_map.68
  9.1 2.3 %collective-permute-done.1.outer_ref = bf16[80,512]{1,0:T(8,128)(2,1)S(1)} collective-permute-done((bf16[80,512]{1,0:T(8,128)(2,1)S(1)}, bf16[80,512]{1,0:T(8,128)(2,1)S(1)}, u32[]{:S(2)}, u32[]{:S(2)}) %collective-permute-start.1) | collective-permute-done | bytes 81952 | tf_op jit(solution)/shard_map/ppermute | solution.py:329
  11.4 1.3 %collective-permute-start.2 = (bf16[512,128]{1,0:T(8,128)(2,1)S(1)}, bf16[512,128]{1,0:T(8,128)(2,1)S(1)}, u32[]{:S(2)}, u32[]{:S(2)}) collective-permute-start(bf16[512,128]{1,0:T(8,128)(2,1)S(1)} %shard_map.69.cot_ref), channel_id=1, source_target_pairs={{0,1},{1,0},{2,3},{3,2},{4,5},{5,4},{6,7},{7,6},{8,9},{9,8},{10,11... | collective-permute-start | bytes 393224 | tf_op jit(solution)/shard_map/ppermute | solution.py:319
  12.8 1.2 %shard_map.70 = (bf16[1152,512]{1,0:T(8,128)(2,1)S(1)}, f32[128,512]{1,0:T(8,128)S(1)}, bf16[256,512]{1,0:T(8,128)(2,1)S(1)}, bf16[512,128]{1,0:T(8,128)(2,1)S(1)}) custom-call(bf16[80,512]{1,0:T(8,128)(2,1)S(1)} %collective-permute-done.inner_ref, bf16[48,512]{1,0:T(8,128)(2,1)S(1)} %get-tuple-element.28.own_ref, ...), custom_call_target="tpu_custom_call" | custom-call | flops 1073741824 | bytes 1048576 | tf_op jit(solution)/shard_map/pallas_call | solution.py:297
  13.9 4.3 %collective-permute-start.3 = (bf16[512,128]{1,0:T(8,128)(2,1)S(1)}, bf16[512,128]{1,0:T(8,128)(2,1)S(1)}, u32[]{:S(2)}, u32[]{:S(2)}) collective-permute-start(bf16[512,128]{1,0:T(8,128)(2,1)S(1)} %get-tuple-element.35.refs_1_), channel_id=1, source_target_pairs={{0,3},{1,2},{2,1},{3,0},{4,7},{5,6},{6,5},{7,4},{8,11},{9,10},{10,... | collective-permute-start | bytes 393224 | tf_op jit(solution)/shard_map/ppermute | solution.py:319
  18.2 0.7 shard_map.73
  19.0 1.3 %collective-permute-start.6 = (bf16[2,64,512]{2,1,0:T(8,128)(2,1)S(1)}, bf16[2,64,512]{2,1,0:T(8,128)(2,1)S(1)}, u32[]{:S(2)}, u32[]{:S(2)}) collective-permute-start(bf16[2,64,512]{2,1,0:T(8,128)(2,1)S(1)} %get-tuple-element.37), channel_id=1, source_target_pairs={{0,1},{1,0},{2,3},{3,2},{4,5},{5,4},{6,7},{7,6},{8,9},{9,8},{10,11... | collective-permute-start | bytes 393224 | tf_op jit(solution)/shard_map/ppermute | solution.py:319
  20.3 1.3 %collective-permute-start.4 = (bf16[256,128]{1,0:T(8,128)(2,1)S(1)}, bf16[256,128]{1,0:T(8,128)(2,1)S(1)}, u32[]{:S(2)}, u32[]{:S(2)}) collective-permute-start(bf16[256,128]{1,0:T(8,128)(2,1)S(1)} %shard_map.71), channel_id=1, source_target_pairs={{0,3},{1,2},{2,1},{3,0},{4,7},{5,6},{6,5},{7,4},{8,11},{9,10},{10,... | collective-permute-start | bytes 196616 | tf_op jit(solution)/shard_map/ppermute | solution.py:319
  21.6 0.5 collective-permute-done.3.in_ref.refs_3_
  22.1 2.1 %collective-permute-start.5 = (bf16[256,128]{1,0:T(8,128)(2,1)S(1)}, bf16[256,128]{1,0:T(8,128)(2,1)S(1)}, u32[]{:S(2)}, u32[]{:S(2)}) collective-permute-start(bf16[256,128]{1,0:T(8,128)(2,1)S(1)} %shard_map.72), channel_id=1, source_target_pairs={{0,1},{1,0},{2,3},{3,2},{4,5},{5,4},{6,7},{7,6},{8,9},{9,8},{10,11... | collective-permute-start | bytes 196616 | tf_op jit(solution)/shard_map/ppermute | solution.py:319
  24.2 2.1 %collective-permute-done.6.refs_7_ = bf16[2,64,512]{2,1,0:T(8,128)(2,1)S(1)} collective-permute-done((bf16[2,64,512]{2,1,0:T(8,128)(2,1)S(1)}, bf16[2,64,512]{2,1,0:T(8,128)(2,1)S(1)}, u32[]{:S(2)}, u32[]{:S(2)}) %collective-permute-start.6) | collective-permute-done | bytes 131104 | tf_op jit(solution)/shard_map/ppermute | solution.py:319
  26.2 1.1 %collective-permute-done.4.refs_4_ = bf16[256,128]{1,0:T(8,128)(2,1)S(1)} collective-permute-done((bf16[256,128]{1,0:T(8,128)(2,1)S(1)}, bf16[256,128]{1,0:T(8,128)(2,1)S(1)}, u32[]{:S(2)}, u32[]{:S(2)}) %collective-permute-start.4) | collective-permute-done | bytes 65568 | tf_op jit(solution)/shard_map/ppermute | solution.py:319
  27.4 0.9 %shard_map.74 = (bf16[256,1024]{1,0:T(8,128)(2,1)S(1)}, bf16[2304,128]{1,0:T(8,128)(2,1)S(1)}, bf16[2304,128]{1,0:T(8,128)(2,1)S(1)}, f32[64,512]{1,0:T(8,128)S(1)}, bf16[64,512]{1,0:T(8,128)(2,1)S(1)}) custom-call(bf16[1152,512]{1,0:T(8,128)(2,1)S(1)} %get-tuple-element.34._.xc_ref.refs_0_, bf16[512,128]{1,0:T(8,128)(2,1)S(1)} %get-tuple-element.35.refs_1_, ...), custom_call_target="tpu_custom_call" | custom-call | flops 1073741824 | bytes 1048576 | tf_op jit(solution)/shard_map/pallas_call | solution.py:297
  28.3 0.1 collective-permute-start.7
  28.4 1.4 %shard_map.75.g1_ref = bf16[64,128]{1,0:T(8,128)(2,1)S(1)} custom-call(bf16[256,1024]{1,0:T(8,128)(2,1)S(1)} %get-tuple-element.40.refs_0_, f32[128,512]{1,0:T(8,128)S(1)} %get-tuple-element.41.refs_1_, bf16[256,512]{1,0:T(8,128)(2,1)S(1)} %get-tuple-element.42.refs_2_, bf16[3456,256]{1,0:T(8,128)(2,1)S(1)} %bitcast.21, ...), custom_call_target="tpu_custom_call" | custom-call | flops 1073741824 | bytes 1048576 | tf_op jit(solution)/shard_map/pallas_call | solution.py:297
  29.8 0.6 collective-permute-done.7.got_ref
  30.3 1.0 %shard_map.76 = bf16[2368,128]{1,0:T(8,128)(2,1)} custom-call(bf16[2304,128]{1,0:T(8,128)(2,1)S(1)} %get-tuple-element.38.keep_ref, bf16[2304,128]{1,0:T(8,128)(2,1)S(1)} %collective-permute-done.7.got_ref, bf16[64,128]{1,0:T(8,128)(2,1)S(1)} %shard_map.75.g1_ref), custom_call_target="tpu_custom_call" | custom-call | flops 1048576 | bytes 1048576 | tf_op jit(solution)/shard_map/pallas_call | solution.py:297
  31.3 14.0 %all-to-all-start = ((bf16[32,37,2,128]{3,2,1,0:T(2,128)(2,1)}), bf16[32,37,2,128]{3,2,1,0:T(2,128)(2,1)S(1)}, u32[]{:S(2)}, u32[]{:S(2)}) async-start(bf16[32,37,2,128]{3,2,1,0:T(2,128)(2,1)} %bitcast.6), calls=%async_computation | async-start | bytes 1212416 | tf_op jit(solution)/shard_map/all_to_all | solution.py:388
  45.3 1.7 %collective-permute-start.8 = (bf16[64,512]{1,0:T(8,128)(2,1)S(1)}, bf16[64,512]{1,0:T(8,128)(2,1)S(1)}, u32[]{:S(2)}, u32[]{:S(2)}) collective-permute-start(bf16[64,512]{1,0:T(8,128)(2,1)S(1)} %get-tuple-element.44), channel_id=1, source_target_pairs={{0,3},{1,2},{2,1},{3,0},{4,7},{5,6},{6,5},{7,4},{8,11},{9,10},{10,... | collective-permute-start | bytes 196616 | tf_op jit(solution)/shard_map/ppermute | solution.py:319
  47.0 8.2 %collective-permute-done.8.refs_2_ = bf16[64,512]{1,0:T(8,128)(2,1)S(1)} collective-permute-done((bf16[64,512]{1,0:T(8,128)(2,1)S(1)}, bf16[64,512]{1,0:T(8,128)(2,1)S(1)}, u32[]{:S(2)}, u32[]{:S(2)}) %collective-permute-start.8) | collective-permute-done | bytes 65568 | tf_op jit(solution)/shard_map/ppermute | solution.py:319
  55.2 0.8 %all-to-all-done = bf16[32,37,2,128]{3,2,1,0:T(2,128)(2,1)S(1)} async-done(((bf16[32,37,2,128]{3,2,1,0:T(2,128)(2,1)}), bf16[32,37,2,128]{3,2,1,0:T(2,128)(2,1)S(1)}, u32[]{:S(2)}, u32[]{:S(2)}) %all-to-all-start) | async-done | bytes 606240 | tf_op jit(solution)/shard_map/all_to_all | solution.py:388
  56.1 0.7 shard_map.77
  56.8 15.0 %all_to_all.10 = bf16[32,37,2,128]{3,2,1,0:T(2,128)(2,1)S(1)} all-to-all(bf16[32,37,2,128]{3,2,1,0:T(2,128)(2,1)S(1)} %bitcast.17), channel_id=1, replica_groups={{0,8,16,24,32,40,48,56,64,72,80,88,96,104,112,120,128,136,144,152,160,1..., dimensions={0} | all-to-all | bytes 1212416 | tf_op jit(solution)/shard_map/all_to_all | solution.py:388
  71.7 3.6 %collective-permute-start.9 = (bf16[2368,128]{1,0:T(8,128)(2,1)S(1)}, bf16[2368,128]{1,0:T(8,128)(2,1)S(1)}, u32[]{:S(2)}, u32[]{:S(2)}) collective-permute-start(bf16[2368,128]{1,0:T(8,128)(2,1)S(1)} %bitcast.15), channel_id=1, source_target_pairs={{0,4},{4,0},{8,12},{12,8},{16,20},{20,16},{24,28},{28,24},{32,36},... | collective-permute-start | bytes 1818632 | tf_op jit(solution)/shard_map/ppermute | solution.py:403
  75.4 1.5 %shard_map.78 = (f32[3,1152,256]{2,1,0:T(8,128)}, bf16[64,128]{1,0:T(8,128)(2,1)S(1)}) custom-call(bf16[2368,128]{1,0:T(8,128)(2,1)S(1)} %bitcast.16), custom_call_target="tpu_custom_call" | custom-call | flops 1048576 | bytes 1048576 | tf_op jit(solution)/shard_map/pallas_call | solution.py:297
  76.9 0.1 collective-permute-done.9.other_ref
  77.0 1.2 %shard_map.79 = (f32[3,1152,256]{2,1,0:T(8,128)}, f32[12,27,32]{2,1,0:T(8,128)}) custom-call(f32[3,1152,256]{2,1,0:T(8,128)} %get-tuple-element.47._, bf16[64,128]{1,0:T(8,128)(2,1)S(1)} %get-tuple-element.48.mine_ref, bf16[2368,128]{1,0:T(8,128)(2,1)S(1)} %collective-permute-done.9.other_ref), custom_call_target="tpu_custom_call", output_to_operand_aliasing={{0}: (0, {})} | custom-call | flops 1048576 | bytes 1048576 | tf_op jit(solution)/shard_map/pallas_call | solution.py:297
  (15 shorter events, 0.2 us)
Async XLA Ops:
  0.6 0.8 %copy-start = (bf16[64,2,2,128]{3,2,1,0:T(2,128)(2,1)S(1)}, bf16[64,2,2,128]{3,2,1,0:T(2,128)(2,1)}, u32[]{:S(2)}) copy-start(bf16[64,2,2,128]{3,2,1,0:T(2,128)(2,1)} %param.7) | copy-start | bytes 196612
  1.5 0.8 %copy-start.1 = (bf16[3,2,8,512]{3,2,1,0:T(8,128)(2,1)S(1)}, bf16[3,2,8,512]{3,2,1,0:T(8,128)(2,1)}, u32[]{:S(2)}) copy-start(bf16[3,2,8,512]{3,2,1,0:T(8,128)(2,1)} %param.4) | copy-start | bytes 147460
  2.3 15.9 %copy-start.2 = (bf16[27,128,256]{2,1,0:T(8,128)(2,1)S(1)}, bf16[27,128,256]{2,1,0:T(8,128)(2,1)}, u32[]{:S(2)}) copy-start(bf16[27,128,256]{2,1,0:T(8,128)(2,1)} %param.6) | copy-start | bytes 5308420
  2.3 6.8 %collective-permute-start = (bf16[80,512]{1,0:T(8,128)(2,1)S(1)}, bf16[80,512]{1,0:T(8,128)(2,1)S(1)}, u32[]{:S(2)}, u32[]{:S(2)}) collective-permute-start(bf16[80,512]{1,0:T(8,128)(2,1)S(1)} %get-tuple-element.27), channel_id=1, source_target_pairs={{0,4},{4,0},{8,12},{12,8},{16,20},{20,16},{24,28},{28,24},{32,36},... | collective-permute-start | bytes 245768 | tf_op jit(solution)/shard_map/ppermute | solution.py:328
  5.6 5.7 %collective-permute-start.1 = (bf16[80,512]{1,0:T(8,128)(2,1)S(1)}, bf16[80,512]{1,0:T(8,128)(2,1)S(1)}, u32[]{:S(2)}, u32[]{:S(2)}) collective-permute-start(bf16[80,512]{1,0:T(8,128)(2,1)S(1)} %get-tuple-element.29), channel_id=1, source_target_pairs={{4,8},{8,4},{12,16},{16,12},{20,24},{24,20},{28,32},{32,28},{36,40... | collective-permute-start | bytes 245768 | tf_op jit(solution)/shard_map/ppermute | solution.py:329
  11.4 8.9 %collective-permute-start.2 = (bf16[512,128]{1,0:T(8,128)(2,1)S(1)}, bf16[512,128]{1,0:T(8,128)(2,1)S(1)}, u32[]{:S(2)}, u32[]{:S(2)}) collective-permute-start(bf16[512,128]{1,0:T(8,128)(2,1)S(1)} %shard_map.69.cot_ref), channel_id=1, source_target_pairs={{0,1},{1,0},{2,3},{3,2},{4,5},{5,4},{6,7},{7,6},{8,9},{9,8},{10,11... | collective-permute-start | bytes 393224 | tf_op jit(solution)/shard_map/ppermute | solution.py:319
  13.9 8.2 %collective-permute-start.3 = (bf16[512,128]{1,0:T(8,128)(2,1)S(1)}, bf16[512,128]{1,0:T(8,128)(2,1)S(1)}, u32[]{:S(2)}, u32[]{:S(2)}) collective-permute-start(bf16[512,128]{1,0:T(8,128)(2,1)S(1)} %get-tuple-element.35.refs_1_), channel_id=1, source_target_pairs={{0,3},{1,2},{2,1},{3,0},{4,7},{5,6},{6,5},{7,4},{8,11},{9,10},{10,... | collective-permute-start | bytes 393224 | tf_op jit(solution)/shard_map/ppermute | solution.py:319
  19.0 7.3 %collective-permute-start.6 = (bf16[2,64,512]{2,1,0:T(8,128)(2,1)S(1)}, bf16[2,64,512]{2,1,0:T(8,128)(2,1)S(1)}, u32[]{:S(2)}, u32[]{:S(2)}) collective-permute-start(bf16[2,64,512]{2,1,0:T(8,128)(2,1)S(1)} %get-tuple-element.37), channel_id=1, source_target_pairs={{0,1},{1,0},{2,3},{3,2},{4,5},{5,4},{6,7},{7,6},{8,9},{9,8},{10,11... | collective-permute-start | bytes 393224 | tf_op jit(solution)/shard_map/ppermute | solution.py:319
  20.3 7.1 %collective-permute-start.4 = (bf16[256,128]{1,0:T(8,128)(2,1)S(1)}, bf16[256,128]{1,0:T(8,128)(2,1)S(1)}, u32[]{:S(2)}, u32[]{:S(2)}) collective-permute-start(bf16[256,128]{1,0:T(8,128)(2,1)S(1)} %shard_map.71), channel_id=1, source_target_pairs={{0,3},{1,2},{2,1},{3,0},{4,7},{5,6},{6,5},{7,4},{8,11},{9,10},{10,... | collective-permute-start | bytes 196616 | tf_op jit(solution)/shard_map/ppermute | solution.py:319
  22.1 5.3 %collective-permute-start.5 = (bf16[256,128]{1,0:T(8,128)(2,1)S(1)}, bf16[256,128]{1,0:T(8,128)(2,1)S(1)}, u32[]{:S(2)}, u32[]{:S(2)}) collective-permute-start(bf16[256,128]{1,0:T(8,128)(2,1)S(1)} %shard_map.72), channel_id=1, source_target_pairs={{0,1},{1,0},{2,3},{3,2},{4,5},{5,4},{6,7},{7,6},{8,9},{9,8},{10,11... | collective-permute-start | bytes 196616 | tf_op jit(solution)/shard_map/ppermute | solution.py:319
  28.3 2.1 %collective-permute-start.7 = (bf16[2304,128]{1,0:T(8,128)(2,1)S(1)}, bf16[2304,128]{1,0:T(8,128)(2,1)S(1)}, u32[]{:S(2)}, u32[]{:S(2)}) collective-permute-start(bf16[2304,128]{1,0:T(8,128)(2,1)S(1)} %get-tuple-element.39), channel_id=1, source_target_pairs={{0,4},{4,0},{8,12},{12,8},{16,20},{20,16},{24,28},{28,24},{32,36},... | collective-permute-start | bytes 1769480 | tf_op jit(solution)/shard_map/ppermute | solution.py:374
  31.3 24.8 %all-to-all-start = ((bf16[32,37,2,128]{3,2,1,0:T(2,128)(2,1)}), bf16[32,37,2,128]{3,2,1,0:T(2,128)(2,1)S(1)}, u32[]{:S(2)}, u32[]{:S(2)}) async-start(bf16[32,37,2,128]{3,2,1,0:T(2,128)(2,1)} %bitcast.6), calls=%async_computation | async-start | bytes 1212416 | tf_op jit(solution)/shard_map/all_to_all | solution.py:388
  45.3 10.0 %collective-permute-start.8 = (bf16[64,512]{1,0:T(8,128)(2,1)S(1)}, bf16[64,512]{1,0:T(8,128)(2,1)S(1)}, u32[]{:S(2)}, u32[]{:S(2)}) collective-permute-start(bf16[64,512]{1,0:T(8,128)(2,1)S(1)} %get-tuple-element.44), channel_id=1, source_target_pairs={{0,3},{1,2},{2,1},{3,0},{4,7},{5,6},{6,5},{7,4},{8,11},{9,10},{10,... | collective-permute-start | bytes 196616 | tf_op jit(solution)/shard_map/ppermute | solution.py:319
  71.7 5.3 %collective-permute-start.9 = (bf16[2368,128]{1,0:T(8,128)(2,1)S(1)}, bf16[2368,128]{1,0:T(8,128)(2,1)S(1)}, u32[]{:S(2)}, u32[]{:S(2)}) collective-permute-start(bf16[2368,128]{1,0:T(8,128)(2,1)S(1)} %bitcast.15), channel_id=1, source_target_pairs={{0,4},{4,0},{8,12},{12,8},{16,20},{20,16},{24,28},{28,24},{32,36},... | collective-permute-start | bytes 1818632 | tf_op jit(solution)/shard_map/ppermute | solution.py:403

commit v2 on v1

--- a/solution.py
+++ b/solution.py
@@ -27,9 +27,9 @@
     m, r, f, tb = at & 15, (at >> 4) & 3, (at >> 6) & 1, at >> 7
     wi = (m * 11) >> 5
     y = 4 * r + 2 * wi + tb + 2
-    for part in range(3):
-        hit = (lane == (m - 3 * wi) * 16 + f * 8 + y - 8 * part) & (m < 12)
-        hit = hit & (y >= 8 * part) & (y < 8 * part + 8)
+    for part, (first, count) in enumerate(((2, 6), (8, 8), (16, 6))):
+        hit = (lane == ((m - 3 * wi) * 2 + f) * count + y - first) & (m < 12)
+        hit = hit & (y >= first) & (y < first + count)
         row_ref[part] = jnp.where(hit, 1.0, 0.0).astype(BF)
     at, lane = iota((128, 256), 0), iota((128, 256), 1)
     c = (at * 57) >> 9
@@ -46,25 +46,40 @@
     return lax.dot_general(a, b, (((ca,), (cb,)), ((), ())), preferred_element_type=F32)
 
 
-def edges_kernel(video_ref, own_ref, inner_ref, outer_ref, video_out, own_out, rows):
+def edges_kernel(
+    video_ref, own_ref, outer_ref, inner_ref, video_out, own_out, rows, pixels, packed
+):
     core = lax.axis_index("band") % 2
     video_out[...] = video_ref[...]
     own_out[...] = own_ref[...]
     rows[...] = own_ref[...].astype(F32)
-    for ref, r in ((inner_ref, 1 - core), (outer_ref, core)):
-        ref[:48, :] = video_ref[...]
-        edge = rows[pl.ds(r, 128, stride=2), :].astype(BF)
-        for i in range(4):
-            ref[48:, i * 128 : i * 128 + 128] = edge[i * 32 : i * 32 + 32, :]
-
-
-def grown_kernel(own_ref, inner_ref, outer_ref, _, __, out_ref):
+    pixels[...] = video_ref[...].astype(F32)
+
+    def put(ref, r):
+        ref[:128, :] = rows[pl.ds(r, 128, stride=2), :].astype(BF)
+        for g in range(6):
+            for i in range(4):
+                packed[i * 36 + g * 6 : i * 36 + g * 6 + 6, :] = pixels[
+                    g * 8 + 2 * r : g * 8 + 2 * r + 6, i * 128 : i * 128 + 128
+                ]
+        ref[128:, :] = packed[...].astype(BF)
+
+    @pl.when(core == 0)
+    def _():
+        put(inner_ref, 1)
+        put(outer_ref, 0)
+
+    @pl.when(core == 1)
+    def _():
+        put(inner_ref, 0)
+        put(outer_ref, 1)
+
+
+def grown_kernel(own_ref, outer_ref, inner_ref, _, __, out_ref):
     core = lax.axis_index("band") % 2
     out_ref[:256, :] = own_ref[...]
     for side, ref in ((1 - core, inner_ref), (core, outer_ref)):
-        for i in range(4):
-            at = pl.multiple_of(256 + side * 128 + i * 32, 32)
-            out_ref[pl.ds(at, 32), :] = ref[48:, i * 128 : i * 128 + 128]
+        out_ref[pl.ds(pl.multiple_of(256 + side * 128, 128), 128), :] = ref[:128, :]
 
 
 def shifted(x, step):
@@ -76,17 +91,21 @@
 
 
 def forward_kernel(
-    inner_ref, own_ref, outer_ref, col_ref, row_ref, sel_ref, w1_ref, cot_ref,
-    xc_ref, pre_ref, win_ref, cot_out, one, two,
+    outer_ref, own_ref, inner_ref, col_ref, row_ref, sel_ref, w1_ref, cot_ref,
+    xc_ref, pre_ref, win_ref, cot_out, one, two, packed,
 ):
     band = lax.axis_index("band")
     core = band % 2
     cot_out[...] = cot_ref[...]
     last = lax.axis_size("band") - 1
+    beyond = []
+    for ref in (inner_ref, outer_ref):
+        packed[...] = ref[128:, :].astype(F32)
+        beyond.append(jnp.concatenate([packed[k * 36 : k * 36 + 36, :] for k in range(4)], 1).astype(BF))
     v = (
-        dot(row_ref[2 - 2 * core][:, :48], inner_ref[:48, :])
+        dot(row_ref[2 - 2 * core][:, :36], beyond[0])
         + dot(row_ref[1, :, :48], own_ref[...])
-        + dot(row_ref[2 * core][:, :48], outer_ref[:48, :])
+        + dot(row_ref[2 * core][:, :36], beyond[1])
     ).astype(BF)
     h = dot(v, col_ref[...])
     top, low = h[:128], h[128:]
@@ -318,15 +337,15 @@
     def swap(x, k):
         return lax.ppermute(x, "chan", [(i, i ^ k) for i in range(4)])
 
-    inner, outer, flat, own = call(
+    outer, inner, flat, own = call(
         edges_kernel,
-        [((80, 512), BF), ((80, 512), BF), ((48, 512), BF), ((256, 128), BF)],
-        [((256, 128), F32)],
+        [((272, 128), BF), ((272, 128), BF), ((48, 512), BF), ((256, 128), BF)],
+        [((256, 128), F32), ((48, 512), F32), ((144, 128), F32)],
         1 << 20,
         flat, own,
     )
+    outer = lax.ppermute(outer, "band", [(i, i + 1 - 2 * (i % 2 == 0)) for i in range(1, n - 1)])
     inner = lax.ppermute(inner, "band", flip)
-    outer = lax.ppermute(outer, "band", [(i, i + 1 - 2 * (i % 2 == 0)) for i in range(1, n - 1)])
     cols, rows, sel = call(
         matrix_kernel,
         [((512, 512), BF), ((3, 256, 128), BF), ((4, 128, 256), BF)],
@@ -336,7 +355,7 @@
     w1 = weight_one[9:].reshape(2, 9, 12, 32).transpose(0, 2, 1, 3).reshape(2, 108, 32)
     w1 = jnp.pad(w1, ((0, 0), (0, 20), (0, 0)))
     (own,) = call(
-        grown_kernel, [((512, 128), BF)], [], 1 << 20, own, inner, outer, sel, w1,
+        grown_kernel, [((512, 128), BF)], [], 1 << 20, own, outer, inner, sel, w1,
         far=(3, 4),
     )
     near = swap(own, 1)
@@ -344,9 +363,9 @@
     xc, pre, win, own = call(
         forward_kernel,
         [((1152, 512), BF), ((128, 512), F32), ((256, 512), BF), ((512, 128), BF)],
-        [((2, 256, 512), BF), ((4, 128, 128), F32)],
+        [((2, 256, 512), BF), ((4, 128, 128), F32), ((144, 128), F32)],
         1 << 30,
-        inner, flat, outer, cols, rows, sel, w1, own,
+        outer, flat, inner, cols, rows, sel, w1, own,
     )
     far = swap(own, 3)
     (near_part,) = call(first_rows_kernel, [((256, 128), BF)], [], 1 << 10, near, xc, far=(1,))

time: 78.6 us -> 78.2 us (level)
  starting transfers between devices: 35 us -> 31.6 us
  waiting for transfers between devices: 15.7 us -> 18.7 us
    ppermute x6, waiting for transfers between devices: 11.9 us -> 17.2 us  [swap(): return lax.ppermute(x, 'chan', [(i, i ^ k) for i in range(4)])]
    all_to_all x1, starting transfers between devices: 14 us -> 9.55 us  [exchange(): x = lax.all_to_all(x, 'band', 0, 0, tiled=True, axis_index_groups=groups)]
    ppermute x1, starting transfers between devices: 3.33 us -> 0.09 us  [on_device(): inner = lax.ppermute(inner, 'band', flip)]
    ppermute x1, starting transfers between devices: 1.91 us -> 4.73 us  [on_device(): lax.ppermute(outer, 'band', [(i, i + 1 - 2 * (i % 2 == 0)) for i in range...]
    ppermute x1, waiting for transfers between devices: 2.25 us -> 0.29 us  [on_device(): lax.ppermute(outer, 'band', [(i, i + 1 - 2 * (i % 2 == 0)) for i in range...]
where the time goes in v2:
time: 78.2 us; the launch traced here: 77.8 us
  starting transfers between devices  31.6 us (40%)
  waiting for transfers between devices  18.7 us (24%)
  blocking collectives  15 us (19%)
  Pallas kernels  9.13 us (12%)
  local copies, waits for them, and re-layouts  2.63 us (3%)
    ppermute x6, waiting for transfers between devices, swap(): return lax.ppermute(x, 'chan', [(i, i ^ k) for i in range(4)])  17.2 us
    all_to_all x1, blocking collectives, exchange(): x = lax.all_to_all(x, 'band', 0, 0, tiled=True, axis_index_groups=groups)  15 us
    ppermute x6, starting transfers between devices, swap(): return lax.ppermute(x, 'chan', [(i, i ^ k) for i in range(4)])  12.8 us
    all_to_all x1, starting transfers between devices, exchange(): x = lax.all_to_all(x, 'band', 0, 0, tiled=True, axis_index_groups=groups)  9.55 us
    pallas_call x13, Pallas kernels, call(): pl.pallas_call(kernel, out_shape=[jax.ShapeDtypeStruct(*o) for o in outs]...  9.13 us
    ppermute x1, starting transfers between devices, on_device(): lax.ppermute(outer, 'band', [(i, i + 1 - 2 * (i % 2 == 0)) for i in range...  4.73 us
    ppermute x1, starting transfers between devices, on_device(): other = lax.ppermute(mine, 'band', flip)  3.64 us
    unnamed x7, local copies, waits for them, and re-layouts  1.65 us
  transfers between devices with their start and end apart: 11, of which 8 were waited for; matrix products, arithmetic and copies ran while one was open for 1% of the time, Pallas kernels for 7%

profile of v2, /device:TPU:1, one launch (start us, length us, event | category | flops | bytes accessed | tf_op | source)
XLA Modules:
  0.0 77.8 jit_solution(6737181530381155455)
XLA Ops:
  0.6 0.8 %copy-done = bf16[64,2,2,128]{3,2,1,0:T(2,128)(2,1)S(1)} copy-done((bf16[64,2,2,128]{3,2,1,0:T(2,128)(2,1)S(1)}, bf16[64,2,2,128]{3,2,1,0:T(2,128)(2,1)}, u32[]{:S(2)}) %copy-start) | copy-done | bytes 65560
  1.5 0.8 %copy-done.1 = bf16[3,2,8,512]{3,2,1,0:T(8,128)(2,1)S(1)} copy-done((bf16[3,2,8,512]{3,2,1,0:T(8,128)(2,1)S(1)}, bf16[3,2,8,512]{3,2,1,0:T(8,128)(2,1)}, u32[]{:S(2)}) %copy-start.1) | copy-done | bytes 49176
  2.3 4.7 %collective-permute-start = (bf16[272,128]{1,0:T(8,128)(2,1)S(1)}, bf16[272,128]{1,0:T(8,128)(2,1)S(1)}, u32[]{:S(2)}, u32[]{:S(2)}) collective-permute-start(bf16[272,128]{1,0:T(8,128)(2,1)S(1)} %get-tuple-element.27), channel_id=1, source_target_pairs={{4,8},{8,4},{12,16},{16,12},{20,24},{24,20},{28,32},{32,28},{36,40... | collective-permute-start | bytes 208904 | tf_op jit(solution)/shard_map/ppermute | solution.py:347
  7.1 0.1 collective-permute-start.1
  7.2 0.9 %slice.3 = bf16[18,12,32]{2,0,1:T(8,128)(2,1)S(1)} slice(bf16[27,12,32]{2,0,1:T(8,128)(2,1)} %param.5), slice={[9:27], [0:12], [0:32]} | slice | bytes 27648 | tf_op jit(solution)/shard_map/slice | solution.py:355
  8.2 0.5 shard_map.68
  8.8 0.3 collective-permute-done.outer_ref
  9.1 3.1 %collective-permute-start.2 = (bf16[512,128]{1,0:T(8,128)(2,1)S(1)}, bf16[512,128]{1,0:T(8,128)(2,1)S(1)}, u32[]{:S(2)}, u32[]{:S(2)}) collective-permute-start(bf16[512,128]{1,0:T(8,128)(2,1)S(1)} %shard_map.69.cot_ref), channel_id=1, source_target_pairs={{0,1},{1,0},{2,3},{3,2},{4,5},{5,4},{6,7},{7,6},{8,9},{9,8},{10,11... | collective-permute-start | bytes 393224 | tf_op jit(solution)/shard_map/ppermute | solution.py:338
  12.2 1.2 %shard_map.70 = (bf16[1152,512]{1,0:T(8,128)(2,1)S(1)}, f32[128,512]{1,0:T(8,128)S(1)}, bf16[256,512]{1,0:T(8,128)(2,1)S(1)}, bf16[512,128]{1,0:T(8,128)(2,1)S(1)}) custom-call(bf16[272,128]{1,0:T(8,128)(2,1)S(1)} %collective-permute-done.outer_ref, bf16[48,512]{1,0:T(8,128)(2,1)S(1)} %get-tuple-element.28.own_ref, ...), custom_call_target="tpu_custom_call" | custom-call | flops 1073741824 | bytes 1048576 | tf_op jit(solution)/shard_map/pallas_call | solution.py:316
  13.3 4.3 %collective-permute-start.3 = (bf16[512,128]{1,0:T(8,128)(2,1)S(1)}, bf16[512,128]{1,0:T(8,128)(2,1)S(1)}, u32[]{:S(2)}, u32[]{:S(2)}) collective-permute-start(bf16[512,128]{1,0:T(8,128)(2,1)S(1)} %get-tuple-element.35.refs_1_), channel_id=1, source_target_pairs={{0,3},{1,2},{2,1},{3,0},{4,7},{5,6},{6,5},{7,4},{8,11},{9,10},{10,... | collective-permute-start | bytes 393224 | tf_op jit(solution)/shard_map/ppermute | solution.py:338
  17.6 0.7 shard_map.73
  18.4 1.3 %collective-permute-start.6 = (bf16[2,64,512]{2,1,0:T(8,128)(2,1)S(1)}, bf16[2,64,512]{2,1,0:T(8,128)(2,1)S(1)}, u32[]{:S(2)}, u32[]{:S(2)}) collective-permute-start(bf16[2,64,512]{2,1,0:T(8,128)(2,1)S(1)} %get-tuple-element.37), channel_id=1, source_target_pairs={{0,1},{1,0},{2,3},{3,2},{4,5},{5,4},{6,7},{7,6},{8,9},{9,8},{10,11... | collective-permute-start | bytes 393224 | tf_op jit(solution)/shard_map/ppermute | solution.py:338
  19.7 1.3 %collective-permute-start.4 = (bf16[256,128]{1,0:T(8,128)(2,1)S(1)}, bf16[256,128]{1,0:T(8,128)(2,1)S(1)}, u32[]{:S(2)}, u32[]{:S(2)}) collective-permute-start(bf16[256,128]{1,0:T(8,128)(2,1)S(1)} %shard_map.71), channel_id=1, source_target_pairs={{0,3},{1,2},{2,1},{3,0},{4,7},{5,6},{6,5},{7,4},{8,11},{9,10},{10,... | collective-permute-start | bytes 196616 | tf_op jit(solution)/shard_map/ppermute | solution.py:338
  21.0 0.1 collective-permute-done.3.in_ref.refs_3_
  21.1 1.4 %collective-permute-start.5 = (bf16[256,128]{1,0:T(8,128)(2,1)S(1)}, bf16[256,128]{1,0:T(8,128)(2,1)S(1)}, u32[]{:S(2)}, u32[]{:S(2)}) collective-permute-start(bf16[256,128]{1,0:T(8,128)(2,1)S(1)} %shard_map.72), channel_id=1, source_target_pairs={{0,1},{1,0},{2,3},{3,2},{4,5},{5,4},{6,7},{7,6},{8,9},{9,8},{10,11... | collective-permute-start | bytes 196616 | tf_op jit(solution)/shard_map/ppermute | solution.py:338
  22.5 3.0 %collective-permute-done.6.refs_7_ = bf16[2,64,512]{2,1,0:T(8,128)(2,1)S(1)} collective-permute-done((bf16[2,64,512]{2,1,0:T(8,128)(2,1)S(1)}, bf16[2,64,512]{2,1,0:T(8,128)(2,1)S(1)}, u32[]{:S(2)}, u32[]{:S(2)}) %collective-permute-start.6) | collective-permute-done | bytes 131104 | tf_op jit(solution)/shard_map/ppermute | solution.py:338
  25.5 5.7 %collective-permute-done.4.refs_4_ = bf16[256,128]{1,0:T(8,128)(2,1)S(1)} collective-permute-done((bf16[256,128]{1,0:T(8,128)(2,1)S(1)}, bf16[256,128]{1,0:T(8,128)(2,1)S(1)}, u32[]{:S(2)}, u32[]{:S(2)}) %collective-permute-start.4) | collective-permute-done | bytes 65568 | tf_op jit(solution)/shard_map/ppermute | solution.py:338
  31.1 0.9 %shard_map.74 = (bf16[256,1024]{1,0:T(8,128)(2,1)S(1)}, bf16[2304,128]{1,0:T(8,128)(2,1)S(1)}, bf16[2304,128]{1,0:T(8,128)(2,1)S(1)}, f32[64,512]{1,0:T(8,128)S(1)}, bf16[64,512]{1,0:T(8,128)(2,1)S(1)}) custom-call(bf16[1152,512]{1,0:T(8,128)(2,1)S(1)} %get-tuple-element.34._.xc_ref.refs_0_, bf16[512,128]{1,0:T(8,128)(2,1)S(1)} %get-tuple-element.35.refs_1_, ...), custom_call_target="tpu_custom_call" | custom-call | flops 1073741824 | bytes 1048576 | tf_op jit(solution)/shard_map/pallas_call | solution.py:316
  32.0 0.8 collective-permute-start.7
  32.8 1.4 %shard_map.75.g1_ref = bf16[64,128]{1,0:T(8,128)(2,1)S(1)} custom-call(bf16[256,1024]{1,0:T(8,128)(2,1)S(1)} %get-tuple-element.40.refs_0_, f32[128,512]{1,0:T(8,128)S(1)} %get-tuple-element.41.refs_1_, bf16[256,512]{1,0:T(8,128)(2,1)S(1)} %get-tuple-element.42.refs_2_, bf16[3456,256]{1,0:T(8,128)(2,1)S(1)} %bitcast.21, ...), custom_call_target="tpu_custom_call" | custom-call | flops 1073741824 | bytes 1048576 | tf_op jit(solution)/shard_map/pallas_call | solution.py:316
  34.2 0.2 collective-permute-done.7.got_ref
  34.4 1.0 %shard_map.76 = bf16[2368,128]{1,0:T(8,128)(2,1)} custom-call(bf16[2304,128]{1,0:T(8,128)(2,1)S(1)} %get-tuple-element.38.keep_ref, bf16[2304,128]{1,0:T(8,128)(2,1)S(1)} %collective-permute-done.7.got_ref, bf16[64,128]{1,0:T(8,128)(2,1)S(1)} %shard_map.75.g1_ref), custom_call_target="tpu_custom_call" | custom-call | flops 1048576 | bytes 1048576 | tf_op jit(solution)/shard_map/pallas_call | solution.py:316
  35.4 9.6 %all-to-all-start = ((bf16[32,37,2,128]{3,2,1,0:T(2,128)(2,1)}), bf16[32,37,2,128]{3,2,1,0:T(2,128)(2,1)S(1)}, u32[]{:S(2)}, u32[]{:S(2)}) async-start(bf16[32,37,2,128]{3,2,1,0:T(2,128)(2,1)} %bitcast.6), calls=%async_computation | async-start | bytes 1212416 | tf_op jit(solution)/shard_map/all_to_all | solution.py:407
  44.9 1.5 %collective-permute-start.8 = (bf16[64,512]{1,0:T(8,128)(2,1)S(1)}, bf16[64,512]{1,0:T(8,128)(2,1)S(1)}, u32[]{:S(2)}, u32[]{:S(2)}) collective-permute-start(bf16[64,512]{1,0:T(8,128)(2,1)S(1)} %get-tuple-element.44), channel_id=1, source_target_pairs={{0,3},{1,2},{2,1},{3,0},{4,7},{5,6},{6,5},{7,4},{8,11},{9,10},{10,... | collective-permute-start | bytes 196616 | tf_op jit(solution)/shard_map/ppermute | solution.py:338
  46.4 8.5 %collective-permute-done.8.refs_2_ = bf16[64,512]{1,0:T(8,128)(2,1)S(1)} collective-permute-done((bf16[64,512]{1,0:T(8,128)(2,1)S(1)}, bf16[64,512]{1,0:T(8,128)(2,1)S(1)}, u32[]{:S(2)}, u32[]{:S(2)}) %collective-permute-start.8) | collective-permute-done | bytes 65568 | tf_op jit(solution)/shard_map/ppermute | solution.py:338
  54.8 0.9 %all-to-all-done = bf16[32,37,2,128]{3,2,1,0:T(2,128)(2,1)S(1)} async-done(((bf16[32,37,2,128]{3,2,1,0:T(2,128)(2,1)}), bf16[32,37,2,128]{3,2,1,0:T(2,128)(2,1)S(1)}, u32[]{:S(2)}, u32[]{:S(2)}) %all-to-all-start) | async-done | bytes 606240 | tf_op jit(solution)/shard_map/all_to_all | solution.py:407
  55.7 0.7 shard_map.77
  56.4 15.0 %all_to_all.10 = bf16[32,37,2,128]{3,2,1,0:T(2,128)(2,1)S(1)} all-to-all(bf16[32,37,2,128]{3,2,1,0:T(2,128)(2,1)S(1)} %bitcast.17), channel_id=1, replica_groups={{0,8,16,24,32,40,48,56,64,72,80,88,96,104,112,120,128,136,144,152,160,1..., dimensions={0} | all-to-all | bytes 1212416 | tf_op jit(solution)/shard_map/all_to_all | solution.py:407
  71.4 3.6 %collective-permute-start.9 = (bf16[2368,128]{1,0:T(8,128)(2,1)S(1)}, bf16[2368,128]{1,0:T(8,128)(2,1)S(1)}, u32[]{:S(2)}, u32[]{:S(2)}) collective-permute-start(bf16[2368,128]{1,0:T(8,128)(2,1)S(1)} %bitcast.15), channel_id=1, source_target_pairs={{0,4},{4,0},{8,12},{12,8},{16,20},{20,16},{24,28},{28,24},{32,36},... | collective-permute-start | bytes 1818632 | tf_op jit(solution)/shard_map/ppermute | solution.py:422
  75.0 1.5 %shard_map.78 = (f32[3,1152,256]{2,1,0:T(8,128)}, bf16[64,128]{1,0:T(8,128)(2,1)S(1)}) custom-call(bf16[2368,128]{1,0:T(8,128)(2,1)S(1)} %bitcast.16), custom_call_target="tpu_custom_call" | custom-call | flops 1048576 | bytes 1048576 | tf_op jit(solution)/shard_map/pallas_call | solution.py:316
  76.5 0.1 collective-permute-done.9.other_ref
  76.6 1.2 %shard_map.79 = (f32[3,1152,256]{2,1,0:T(8,128)}, f32[12,27,32]{2,1,0:T(8,128)}) custom-call(f32[3,1152,256]{2,1,0:T(8,128)} %get-tuple-element.47._, bf16[64,128]{1,0:T(8,128)(2,1)S(1)} %get-tuple-element.48.mine_ref, bf16[2368,128]{1,0:T(8,128)(2,1)S(1)} %collective-permute-done.9.other_ref), custom_call_target="tpu_custom_call", output_to_operand_aliasing={{0}: (0, {})} | custom-call | flops 1048576 | bytes 1048576 | tf_op jit(solution)/shard_map/pallas_call | solution.py:316
  (15 shorter events, 0.2 us)
Async XLA Ops:
  0.6 0.8 %copy-start = (bf16[64,2,2,128]{3,2,1,0:T(2,128)(2,1)S(1)}, bf16[64,2,2,128]{3,2,1,0:T(2,128)(2,1)}, u32[]{:S(2)}) copy-start(bf16[64,2,2,128]{3,2,1,0:T(2,128)(2,1)} %param.7) | copy-start | bytes 196612
  1.5 0.8 %copy-start.1 = (bf16[3,2,8,512]{3,2,1,0:T(8,128)(2,1)S(1)}, bf16[3,2,8,512]{3,2,1,0:T(8,128)(2,1)}, u32[]{:S(2)}) copy-start(bf16[3,2,8,512]{3,2,1,0:T(8,128)(2,1)} %param.4) | copy-start | bytes 147460
  2.3 15.4 %copy-start.2 = (bf16[27,128,256]{2,1,0:T(8,128)(2,1)S(1)}, bf16[27,128,256]{2,1,0:T(8,128)(2,1)}, u32[]{:S(2)}) copy-start(bf16[27,128,256]{2,1,0:T(8,128)(2,1)} %param.6) | copy-start | bytes 5308420
  2.3 6.7 %collective-permute-start = (bf16[272,128]{1,0:T(8,128)(2,1)S(1)}, bf16[272,128]{1,0:T(8,128)(2,1)S(1)}, u32[]{:S(2)}, u32[]{:S(2)}) collective-permute-start(bf16[272,128]{1,0:T(8,128)(2,1)S(1)} %get-tuple-element.27), channel_id=1, source_target_pairs={{4,8},{8,4},{12,16},{16,12},{20,24},{24,20},{28,32},{32,28},{36,40... | collective-permute-start | bytes 208904 | tf_op jit(solution)/shard_map/ppermute | solution.py:347
  7.1 2.0 %collective-permute-start.1 = (bf16[272,128]{1,0:T(8,128)(2,1)S(1)}, bf16[272,128]{1,0:T(8,128)(2,1)S(1)}, u32[]{:S(2)}, u32[]{:S(2)}) collective-permute-start(bf16[272,128]{1,0:T(8,128)(2,1)S(1)} %get-tuple-element.29), channel_id=1, source_target_pairs={{0,4},{4,0},{8,12},{12,8},{16,20},{20,16},{24,28},{28,24},{32,36},... | collective-permute-start | bytes 208904 | tf_op jit(solution)/shard_map/ppermute | solution.py:348
  9.1 10.6 %collective-permute-start.2 = (bf16[512,128]{1,0:T(8,128)(2,1)S(1)}, bf16[512,128]{1,0:T(8,128)(2,1)S(1)}, u32[]{:S(2)}, u32[]{:S(2)}) collective-permute-start(bf16[512,128]{1,0:T(8,128)(2,1)S(1)} %shard_map.69.cot_ref), channel_id=1, source_target_pairs={{0,1},{1,0},{2,3},{3,2},{4,5},{5,4},{6,7},{7,6},{8,9},{9,8},{10,11... | collective-permute-start | bytes 393224 | tf_op jit(solution)/shard_map/ppermute | solution.py:338
  13.3 7.7 %collective-permute-start.3 = (bf16[512,128]{1,0:T(8,128)(2,1)S(1)}, bf16[512,128]{1,0:T(8,128)(2,1)S(1)}, u32[]{:S(2)}, u32[]{:S(2)}) collective-permute-start(bf16[512,128]{1,0:T(8,128)(2,1)S(1)} %get-tuple-element.35.refs_1_), channel_id=1, source_target_pairs={{0,3},{1,2},{2,1},{3,0},{4,7},{5,6},{6,5},{7,4},{8,11},{9,10},{10,... | collective-permute-start | bytes 393224 | tf_op jit(solution)/shard_map/ppermute | solution.py:338
  18.4 7.1 %collective-permute-start.6 = (bf16[2,64,512]{2,1,0:T(8,128)(2,1)S(1)}, bf16[2,64,512]{2,1,0:T(8,128)(2,1)S(1)}, u32[]{:S(2)}, u32[]{:S(2)}) collective-permute-start(bf16[2,64,512]{2,1,0:T(8,128)(2,1)S(1)} %get-tuple-element.37), channel_id=1, source_target_pairs={{0,1},{1,0},{2,3},{3,2},{4,5},{5,4},{6,7},{7,6},{8,9},{9,8},{10,11... | collective-permute-start | bytes 393224 | tf_op jit(solution)/shard_map/ppermute | solution.py:338
  19.7 11.5 %collective-permute-start.4 = (bf16[256,128]{1,0:T(8,128)(2,1)S(1)}, bf16[256,128]{1,0:T(8,128)(2,1)S(1)}, u32[]{:S(2)}, u32[]{:S(2)}) collective-permute-start(bf16[256,128]{1,0:T(8,128)(2,1)S(1)} %shard_map.71), channel_id=1, source_target_pairs={{0,3},{1,2},{2,1},{3,0},{4,7},{5,6},{6,5},{7,4},{8,11},{9,10},{10,... | collective-permute-start | bytes 196616 | tf_op jit(solution)/shard_map/ppermute | solution.py:338
  21.1 10.1 %collective-permute-start.5 = (bf16[256,128]{1,0:T(8,128)(2,1)S(1)}, bf16[256,128]{1,0:T(8,128)(2,1)S(1)}, u32[]{:S(2)}, u32[]{:S(2)}) collective-permute-start(bf16[256,128]{1,0:T(8,128)(2,1)S(1)} %shard_map.72), channel_id=1, source_target_pairs={{0,1},{1,0},{2,3},{3,2},{4,5},{5,4},{6,7},{7,6},{8,9},{9,8},{10,11... | collective-permute-start | bytes 196616 | tf_op jit(solution)/shard_map/ppermute | solution.py:338
  32.0 2.4 %collective-permute-start.7 = (bf16[2304,128]{1,0:T(8,128)(2,1)S(1)}, bf16[2304,128]{1,0:T(8,128)(2,1)S(1)}, u32[]{:S(2)}, u32[]{:S(2)}) collective-permute-start(bf16[2304,128]{1,0:T(8,128)(2,1)S(1)} %get-tuple-element.39), channel_id=1, source_target_pairs={{0,4},{4,0},{8,12},{12,8},{16,20},{20,16},{24,28},{28,24},{32,36},... | collective-permute-start | bytes 1769480 | tf_op jit(solution)/shard_map/ppermute | solution.py:393
  35.4 20.4 %all-to-all-start = ((bf16[32,37,2,128]{3,2,1,0:T(2,128)(2,1)}), bf16[32,37,2,128]{3,2,1,0:T(2,128)(2,1)S(1)}, u32[]{:S(2)}, u32[]{:S(2)}) async-start(bf16[32,37,2,128]{3,2,1,0:T(2,128)(2,1)} %bitcast.6), calls=%async_computation | async-start | bytes 1212416 | tf_op jit(solution)/shard_map/all_to_all | solution.py:407
  44.9 9.9 %collective-permute-start.8 = (bf16[64,512]{1,0:T(8,128)(2,1)S(1)}, bf16[64,512]{1,0:T(8,128)(2,1)S(1)}, u32[]{:S(2)}, u32[]{:S(2)}) collective-permute-start(bf16[64,512]{1,0:T(8,128)(2,1)S(1)} %get-tuple-element.44), channel_id=1, source_target_pairs={{0,3},{1,2},{2,1},{3,0},{4,7},{5,6},{6,5},{7,4},{8,11},{9,10},{10,... | collective-permute-start | bytes 196616 | tf_op jit(solution)/shard_map/ppermute | solution.py:338
  71.4 5.3 %collective-permute-start.9 = (bf16[2368,128]{1,0:T(8,128)(2,1)S(1)}, bf16[2368,128]{1,0:T(8,128)(2,1)S(1)}, u32[]{:S(2)}, u32[]{:S(2)}) collective-permute-start(bf16[2368,128]{1,0:T(8,128)(2,1)S(1)} %bitcast.15), channel_id=1, source_target_pairs={{0,4},{4,0},{8,12},{12,8},{16,20},{20,16},{24,28},{28,24},{32,36},... | collective-permute-start | bytes 1818632 | tf_op jit(solution)/shard_map/ppermute | solution.py:422

commit v3 on v2

--- a/solution.py
+++ b/solution.py
@@ -53,7 +53,7 @@
     video_out[...] = video_ref[...]
     own_out[...] = own_ref[...]
     rows[...] = own_ref[...].astype(F32)
-    pixels[...] = video_ref[...].astype(F32)
+    pixels[:48, :] = video_ref[...].astype(F32)
 
     def put(ref, r):
         ref[:128, :] = rows[pl.ds(r, 128, stride=2), :].astype(BF)
@@ -62,7 +62,7 @@
                 packed[i * 36 + g * 6 : i * 36 + g * 6 + 6, :] = pixels[
                     g * 8 + 2 * r : g * 8 + 2 * r + 6, i * 128 : i * 128 + 128
                 ]
-        ref[128:, :] = packed[...].astype(BF)
+        ref[128:, :] = packed[:144, :].astype(BF)
 
     @pl.when(core == 0)
     def _():
@@ -100,7 +100,7 @@
     last = lax.axis_size("band") - 1
     beyond = []
     for ref in (inner_ref, outer_ref):
-        packed[...] = ref[128:, :].astype(F32)
+        packed[:144, :] = ref[128:, :].astype(F32)
         beyond.append(jnp.concatenate([packed[k * 36 : k * 36 + 36, :] for k in range(4)], 1).astype(BF))
     v = (
         dot(row_ref[2 - 2 * core][:, :36], beyond[0])
@@ -261,13 +261,13 @@
     total = got_ref[:block, :].astype(F32)
     for i in range(block, count * size, block):
         total = total + got_ref[i : i + block, :].astype(F32)
-    wide[...] = total
+    wide[:block, :] = total
     total = wide[:size, :]
     for i in range(1, bunch):
         total = total + wide[i * size : i * size + size, :]
     for i in range(bunch):
         wide[i * size : i * size + size, :] = total
-    total = wide[...].astype(BF)
+    total = wide[:block, :].astype(BF)
     for i in range(0, count * size, block):
         out_ref[i : i + block, :] = total
 
@@ -295,14 +295,16 @@
         copy.wait()
 
 
-def other_half_kernel(_, mine_ref, other_ref, g2_ref, g1_ref, half, taps_s, sems):
+def other_half_kernel(_, mine_ref, other_ref, g2_ref, g1_ref, half, taps_s, stage, sems):
     core = lax.axis_index("band") % 2
     both = mine_ref[...].astype(F32) + other_ref[2304:2368, :].astype(F32)
-    taps_s[...] = jnp.zeros((12, 27, 32), F32)
-    for a in range(2):
-        taps = jnp.transpose(both[32 * a : 32 * a + 32, :])
-        for c in range(12):
-            taps_s[c, 9 * a + 9 : 9 * a + 18, :] = taps[9 * c : 9 * c + 9, :]
+    taps = [jnp.transpose(both[32 * a : 32 * a + 32, :]) for a in range(2)]
+    stage[...] = jnp.zeros((12, 48, 32), F32)
+    for c in range(12):
+        for a in range(2):
+            stage[c, 9 * a + 9 : 9 * a + 18, :] = taps[a][9 * c : 9 * c + 9, :]
+    for c in range(12):
+        taps_s[c] = stage[c, :27, :]
     first = pltpu.make_async_copy(taps_s, g1_ref, sems.at[3])
     first.start()
     for copy in [first] + widen(other_ref, half, g2_ref.at[2 - core], sems, 0):
@@ -340,7 +342,7 @@
     outer, inner, flat, own = call(
         edges_kernel,
         [((272, 128), BF), ((272, 128), BF), ((48, 512), BF), ((256, 128), BF)],
-        [((256, 128), F32), ((48, 512), F32), ((144, 128), F32)],
+        [((256, 128), F32), ((64, 512), F32), ((160, 128), F32)],
         1 << 20,
         flat, own,
     )
@@ -363,7 +365,7 @@
     xc, pre, win, own = call(
         forward_kernel,
         [((1152, 512), BF), ((128, 512), F32), ((256, 512), BF), ((512, 128), BF)],
-        [((2, 256, 512), BF), ((4, 128, 128), F32), ((144, 128), F32)],
+        [((2, 256, 512), BF), ((4, 128, 128), F32), ((160, 128), F32)],
         1 << 30,
         outer, flat, inner, cols, rows, sel, w1, own,
     )
@@ -414,7 +416,7 @@
     mine, latent = call(
         share,
         [((2368, 128), BF), ((256, 128), BF)],
-        [((256, 128), F32), ((2368 // half * min(half, 8), 128), F32)],
+        [((256, 128), F32), ((2368 // half * min(half, 8) + 16, 128), F32)],
         1 << 20,
         part, lat_own, lat_got,
     )
@@ -431,7 +433,7 @@
     g2, g1 = call(
         other_half_kernel,
         [((3, 1152, 256), F32), ((12, 27, 32), F32)],
-        [((1152, 256), F32), ((12, 27, 32), F32), pltpu.SemaphoreType.DMA((4,))],
+        [((1152, 256), F32), ((12, 27, 32), F32), ((12, 48, 32), F32), pltpu.SemaphoreType.DMA((4,))],
         1 << 20,
         g2, g1, other,
         far=(0,), far_out=(0, 1), aliases={0: 0},

time: 78.2 us -> 78.2 us (level)
  no operation moved by 1% of the time
where the time goes in v3:
time: 78.2 us; the launch traced here: 77.9 us
  starting transfers between devices  31.6 us (40%)
  waiting for transfers between devices  18.7 us (24%)
  blocking collectives  15 us (19%)
  Pallas kernels  9.16 us (12%)
  local copies, waits for them, and re-layouts  2.63 us (3%)
    ppermute x6, waiting for transfers between devices, swap(): return lax.ppermute(x, 'chan', [(i, i ^ k) for i in range(4)])  17.2 us
    all_to_all x1, blocking collectives, exchange(): x = lax.all_to_all(x, 'band', 0, 0, tiled=True, axis_index_groups=groups)  15 us
    ppermute x6, starting transfers between devices, swap(): return lax.ppermute(x, 'chan', [(i, i ^ k) for i in range(4)])  12.8 us
    all_to_all x1, starting transfers between devices, exchange(): x = lax.all_to_all(x, 'band', 0, 0, tiled=True, axis_index_groups=groups)  9.56 us
    pallas_call x13, Pallas kernels, call(): pl.pallas_call(kernel, out_shape=[jax.ShapeDtypeStruct(*o) for o in outs]...  9.16 us
    ppermute x1, starting transfers between devices, on_device(): lax.ppermute(outer, 'band', [(i, i + 1 - 2 * (i % 2 == 0)) for i in range...  4.73 us
    ppermute x1, starting transfers between devices, on_device(): other = lax.ppermute(mine, 'band', flip)  3.64 us
    unnamed x7, local copies, waits for them, and re-layouts  1.65 us
  transfers between devices with their start and end apart: 11, of which 8 were waited for; matrix products, arithmetic and copies ran while one was open for 1% of the time, Pallas kernels for 7%

profile of v3, /device:TPU:1, one launch (start us, length us, event | category | flops | bytes accessed | tf_op | source)
XLA Modules:
  0.0 77.9 jit_solution(13212087791901732278)
XLA Ops:
  0.6 0.8 %copy-done = bf16[64,2,2,128]{3,2,1,0:T(2,128)(2,1)S(1)} copy-done((bf16[64,2,2,128]{3,2,1,0:T(2,128)(2,1)S(1)}, bf16[64,2,2,128]{3,2,1,0:T(2,128)(2,1)}, u32[]{:S(2)}) %copy-start) | copy-done | bytes 65560
  1.5 0.8 %copy-done.1 = bf16[3,2,8,512]{3,2,1,0:T(8,128)(2,1)S(1)} copy-done((bf16[3,2,8,512]{3,2,1,0:T(8,128)(2,1)S(1)}, bf16[3,2,8,512]{3,2,1,0:T(8,128)(2,1)}, u32[]{:S(2)}) %copy-start.1) | copy-done | bytes 49176
  2.3 0.1 shard_map.67
  2.3 4.7 %collective-permute-start = (bf16[272,128]{1,0:T(8,128)(2,1)S(1)}, bf16[272,128]{1,0:T(8,128)(2,1)S(1)}, u32[]{:S(2)}, u32[]{:S(2)}) collective-permute-start(bf16[272,128]{1,0:T(8,128)(2,1)S(1)} %get-tuple-element.27), channel_id=1, source_target_pairs={{4,8},{8,4},{12,16},{16,12},{20,24},{24,20},{28,32},{32,28},{36,40... | collective-permute-start | bytes 208904 | tf_op jit(solution)/shard_map/ppermute | solution.py:349
  7.1 0.1 collective-permute-start.1
  7.2 0.9 %slice.3 = bf16[18,12,32]{2,0,1:T(8,128)(2,1)S(1)} slice(bf16[27,12,32]{2,0,1:T(8,128)(2,1)} %param.5), slice={[9:27], [0:12], [0:32]} | slice | bytes 27648 | tf_op jit(solution)/shard_map/slice | solution.py:357
  8.2 0.5 shard_map.68
  8.8 0.3 collective-permute-done.outer_ref
  9.1 3.1 %collective-permute-start.2 = (bf16[512,128]{1,0:T(8,128)(2,1)S(1)}, bf16[512,128]{1,0:T(8,128)(2,1)S(1)}, u32[]{:S(2)}, u32[]{:S(2)}) collective-permute-start(bf16[512,128]{1,0:T(8,128)(2,1)S(1)} %shard_map.69.cot_ref), channel_id=1, source_target_pairs={{0,1},{1,0},{2,3},{3,2},{4,5},{5,4},{6,7},{7,6},{8,9},{9,8},{10,11... | collective-permute-start | bytes 393224 | tf_op jit(solution)/shard_map/ppermute | solution.py:340
  12.2 1.2 %shard_map.70 = (bf16[1152,512]{1,0:T(8,128)(2,1)S(1)}, f32[128,512]{1,0:T(8,128)S(1)}, bf16[256,512]{1,0:T(8,128)(2,1)S(1)}, bf16[512,128]{1,0:T(8,128)(2,1)S(1)}) custom-call(bf16[272,128]{1,0:T(8,128)(2,1)S(1)} %collective-permute-done.outer_ref, bf16[48,512]{1,0:T(8,128)(2,1)S(1)} %get-tuple-element.28.own_ref, ...), custom_call_target="tpu_custom_call" | custom-call | flops 1073741824 | bytes 1048576 | tf_op jit(solution)/shard_map/pallas_call | solution.py:318
  13.3 4.3 %collective-permute-start.3 = (bf16[512,128]{1,0:T(8,128)(2,1)S(1)}, bf16[512,128]{1,0:T(8,128)(2,1)S(1)}, u32[]{:S(2)}, u32[]{:S(2)}) collective-permute-start(bf16[512,128]{1,0:T(8,128)(2,1)S(1)} %get-tuple-element.35.refs_1_), channel_id=1, source_target_pairs={{0,3},{1,2},{2,1},{3,0},{4,7},{5,6},{6,5},{7,4},{8,11},{9,10},{10,... | collective-permute-start | bytes 393224 | tf_op jit(solution)/shard_map/ppermute | solution.py:340
  17.6 0.7 shard_map.73
  18.4 1.3 %collective-permute-start.6 = (bf16[2,64,512]{2,1,0:T(8,128)(2,1)S(1)}, bf16[2,64,512]{2,1,0:T(8,128)(2,1)S(1)}, u32[]{:S(2)}, u32[]{:S(2)}) collective-permute-start(bf16[2,64,512]{2,1,0:T(8,128)(2,1)S(1)} %get-tuple-element.37), channel_id=1, source_target_pairs={{0,1},{1,0},{2,3},{3,2},{4,5},{5,4},{6,7},{7,6},{8,9},{9,8},{10,11... | collective-permute-start | bytes 393224 | tf_op jit(solution)/shard_map/ppermute | solution.py:340
  19.7 1.3 %collective-permute-start.4 = (bf16[256,128]{1,0:T(8,128)(2,1)S(1)}, bf16[256,128]{1,0:T(8,128)(2,1)S(1)}, u32[]{:S(2)}, u32[]{:S(2)}) collective-permute-start(bf16[256,128]{1,0:T(8,128)(2,1)S(1)} %shard_map.71), channel_id=1, source_target_pairs={{0,3},{1,2},{2,1},{3,0},{4,7},{5,6},{6,5},{7,4},{8,11},{9,10},{10,... | collective-permute-start | bytes 196616 | tf_op jit(solution)/shard_map/ppermute | solution.py:340
  21.1 1.4 %collective-permute-start.5 = (bf16[256,128]{1,0:T(8,128)(2,1)S(1)}, bf16[256,128]{1,0:T(8,128)(2,1)S(1)}, u32[]{:S(2)}, u32[]{:S(2)}) collective-permute-start(bf16[256,128]{1,0:T(8,128)(2,1)S(1)} %shard_map.72), channel_id=1, source_target_pairs={{0,1},{1,0},{2,3},{3,2},{4,5},{5,4},{6,7},{7,6},{8,9},{9,8},{10,11... | collective-permute-start | bytes 196616 | tf_op jit(solution)/shard_map/ppermute | solution.py:340
  22.5 3.0 %collective-permute-done.6.refs_7_ = bf16[2,64,512]{2,1,0:T(8,128)(2,1)S(1)} collective-permute-done((bf16[2,64,512]{2,1,0:T(8,128)(2,1)S(1)}, bf16[2,64,512]{2,1,0:T(8,128)(2,1)S(1)}, u32[]{:S(2)}, u32[]{:S(2)}) %collective-permute-start.6) | collective-permute-done | bytes 131104 | tf_op jit(solution)/shard_map/ppermute | solution.py:340
  25.5 5.6 %collective-permute-done.4.refs_4_ = bf16[256,128]{1,0:T(8,128)(2,1)S(1)} collective-permute-done((bf16[256,128]{1,0:T(8,128)(2,1)S(1)}, bf16[256,128]{1,0:T(8,128)(2,1)S(1)}, u32[]{:S(2)}, u32[]{:S(2)}) %collective-permute-start.4) | collective-permute-done | bytes 65568 | tf_op jit(solution)/shard_map/ppermute | solution.py:340
  31.1 0.9 %shard_map.74 = (bf16[256,1024]{1,0:T(8,128)(2,1)S(1)}, bf16[2304,128]{1,0:T(8,128)(2,1)S(1)}, bf16[2304,128]{1,0:T(8,128)(2,1)S(1)}, f32[64,512]{1,0:T(8,128)S(1)}, bf16[64,512]{1,0:T(8,128)(2,1)S(1)}) custom-call(bf16[1152,512]{1,0:T(8,128)(2,1)S(1)} %get-tuple-element.34._.xc_ref.refs_0_, bf16[512,128]{1,0:T(8,128)(2,1)S(1)} %get-tuple-element.35.refs_1_, ...), custom_call_target="tpu_custom_call" | custom-call | flops 1073741824 | bytes 1048576 | tf_op jit(solution)/shard_map/pallas_call | solution.py:318
  32.0 0.8 collective-permute-start.7
  32.8 1.4 %shard_map.75.g1_ref = bf16[64,128]{1,0:T(8,128)(2,1)S(1)} custom-call(bf16[256,1024]{1,0:T(8,128)(2,1)S(1)} %get-tuple-element.40.refs_0_, f32[128,512]{1,0:T(8,128)S(1)} %get-tuple-element.41.refs_1_, bf16[256,512]{1,0:T(8,128)(2,1)S(1)} %get-tuple-element.42.refs_2_, bf16[3456,256]{1,0:T(8,128)(2,1)S(1)} %bitcast.21, ...), custom_call_target="tpu_custom_call" | custom-call | flops 1073741824 | bytes 1048576 | tf_op jit(solution)/shard_map/pallas_call | solution.py:318
  34.2 0.2 collective-permute-done.7.got_ref
  34.4 1.0 %shard_map.76 = bf16[2368,128]{1,0:T(8,128)(2,1)} custom-call(bf16[2304,128]{1,0:T(8,128)(2,1)S(1)} %get-tuple-element.38.keep_ref, bf16[2304,128]{1,0:T(8,128)(2,1)S(1)} %collective-permute-done.7.got_ref, bf16[64,128]{1,0:T(8,128)(2,1)S(1)} %shard_map.75.g1_ref), custom_call_target="tpu_custom_call" | custom-call | flops 1048576 | bytes 1048576 | tf_op jit(solution)/shard_map/pallas_call | solution.py:318
  35.3 9.6 %all-to-all-start = ((bf16[32,37,2,128]{3,2,1,0:T(2,128)(2,1)}), bf16[32,37,2,128]{3,2,1,0:T(2,128)(2,1)S(1)}, u32[]{:S(2)}, u32[]{:S(2)}) async-start(bf16[32,37,2,128]{3,2,1,0:T(2,128)(2,1)} %bitcast.6), calls=%async_computation | async-start | bytes 1212416 | tf_op jit(solution)/shard_map/all_to_all | solution.py:409
  44.9 1.5 %collective-permute-start.8 = (bf16[64,512]{1,0:T(8,128)(2,1)S(1)}, bf16[64,512]{1,0:T(8,128)(2,1)S(1)}, u32[]{:S(2)}, u32[]{:S(2)}) collective-permute-start(bf16[64,512]{1,0:T(8,128)(2,1)S(1)} %get-tuple-element.44), channel_id=1, source_target_pairs={{0,3},{1,2},{2,1},{3,0},{4,7},{5,6},{6,5},{7,4},{8,11},{9,10},{10,... | collective-permute-start | bytes 196616 | tf_op jit(solution)/shard_map/ppermute | solution.py:340
  46.4 8.5 %collective-permute-done.8.refs_2_ = bf16[64,512]{1,0:T(8,128)(2,1)S(1)} collective-permute-done((bf16[64,512]{1,0:T(8,128)(2,1)S(1)}, bf16[64,512]{1,0:T(8,128)(2,1)S(1)}, u32[]{:S(2)}, u32[]{:S(2)}) %collective-permute-start.8) | collective-permute-done | bytes 65568 | tf_op jit(solution)/shard_map/ppermute | solution.py:340
  54.8 0.9 %all-to-all-done = bf16[32,37,2,128]{3,2,1,0:T(2,128)(2,1)S(1)} async-done(((bf16[32,37,2,128]{3,2,1,0:T(2,128)(2,1)}), bf16[32,37,2,128]{3,2,1,0:T(2,128)(2,1)S(1)}, u32[]{:S(2)}, u32[]{:S(2)}) %all-to-all-start) | async-done | bytes 606240 | tf_op jit(solution)/shard_map/all_to_all | solution.py:409
  55.7 0.7 shard_map.77
  56.4 15.0 %all_to_all.10 = bf16[32,37,2,128]{3,2,1,0:T(2,128)(2,1)S(1)} all-to-all(bf16[32,37,2,128]{3,2,1,0:T(2,128)(2,1)S(1)} %bitcast.17), channel_id=1, replica_groups={{0,8,16,24,32,40,48,56,64,72,80,88,96,104,112,120,128,136,144,152,160,1..., dimensions={0} | all-to-all | bytes 1212416 | tf_op jit(solution)/shard_map/all_to_all | solution.py:409
  71.4 3.6 %collective-permute-start.9 = (bf16[2368,128]{1,0:T(8,128)(2,1)S(1)}, bf16[2368,128]{1,0:T(8,128)(2,1)S(1)}, u32[]{:S(2)}, u32[]{:S(2)}) collective-permute-start(bf16[2368,128]{1,0:T(8,128)(2,1)S(1)} %bitcast.15), channel_id=1, source_target_pairs={{0,4},{4,0},{8,12},{12,8},{16,20},{20,16},{24,28},{28,24},{32,36},... | collective-permute-start | bytes 1818632 | tf_op jit(solution)/shard_map/ppermute | solution.py:424
  75.0 1.5 %shard_map.78 = (f32[3,1152,256]{2,1,0:T(8,128)}, bf16[64,128]{1,0:T(8,128)(2,1)S(1)}) custom-call(bf16[2368,128]{1,0:T(8,128)(2,1)S(1)} %bitcast.16), custom_call_target="tpu_custom_call" | custom-call | flops 1048576 | bytes 1048576 | tf_op jit(solution)/shard_map/pallas_call | solution.py:318
  76.5 0.1 collective-permute-done.9.other_ref
  76.6 1.2 %shard_map.79 = (f32[3,1152,256]{2,1,0:T(8,128)}, f32[12,27,32]{2,1,0:T(8,128)}) custom-call(f32[3,1152,256]{2,1,0:T(8,128)} %get-tuple-element.47._, bf16[64,128]{1,0:T(8,128)(2,1)S(1)} %get-tuple-element.48.mine_ref, bf16[2368,128]{1,0:T(8,128)(2,1)S(1)} %collective-permute-done.9.other_ref), custom_call_target="tpu_custom_call", output_to_operand_aliasing={{0}: (0, {})} | custom-call | flops 1048576 | bytes 1048576 | tf_op jit(solution)/shard_map/pallas_call | solution.py:318
  (15 shorter events, 0.2 us)
Async XLA Ops:
  0.6 0.8 %copy-start = (bf16[64,2,2,128]{3,2,1,0:T(2,128)(2,1)S(1)}, bf16[64,2,2,128]{3,2,1,0:T(2,128)(2,1)}, u32[]{:S(2)}) copy-start(bf16[64,2,2,128]{3,2,1,0:T(2,128)(2,1)} %param.7) | copy-start | bytes 196612
  1.5 0.8 %copy-start.1 = (bf16[3,2,8,512]{3,2,1,0:T(8,128)(2,1)S(1)}, bf16[3,2,8,512]{3,2,1,0:T(8,128)(2,1)}, u32[]{:S(2)}) copy-start(bf16[3,2,8,512]{3,2,1,0:T(8,128)(2,1)} %param.4) | copy-start | bytes 147460
  2.3 15.4 %copy-start.2 = (bf16[27,128,256]{2,1,0:T(8,128)(2,1)S(1)}, bf16[27,128,256]{2,1,0:T(8,128)(2,1)}, u32[]{:S(2)}) copy-start(bf16[27,128,256]{2,1,0:T(8,128)(2,1)} %param.6) | copy-start | bytes 5308420
  2.3 6.7 %collective-permute-start = (bf16[272,128]{1,0:T(8,128)(2,1)S(1)}, bf16[272,128]{1,0:T(8,128)(2,1)S(1)}, u32[]{:S(2)}, u32[]{:S(2)}) collective-permute-start(bf16[272,128]{1,0:T(8,128)(2,1)S(1)} %get-tuple-element.27), channel_id=1, source_target_pairs={{4,8},{8,4},{12,16},{16,12},{20,24},{24,20},{28,32},{32,28},{36,40... | collective-permute-start | bytes 208904 | tf_op jit(solution)/shard_map/ppermute | solution.py:349
  7.1 2.0 %collective-permute-start.1 = (bf16[272,128]{1,0:T(8,128)(2,1)S(1)}, bf16[272,128]{1,0:T(8,128)(2,1)S(1)}, u32[]{:S(2)}, u32[]{:S(2)}) collective-permute-start(bf16[272,128]{1,0:T(8,128)(2,1)S(1)} %get-tuple-element.29), channel_id=1, source_target_pairs={{0,4},{4,0},{8,12},{12,8},{16,20},{20,16},{24,28},{28,24},{32,36},... | collective-permute-start | bytes 208904 | tf_op jit(solution)/shard_map/ppermute | solution.py:350
  9.1 10.6 %collective-permute-start.2 = (bf16[512,128]{1,0:T(8,128)(2,1)S(1)}, bf16[512,128]{1,0:T(8,128)(2,1)S(1)}, u32[]{:S(2)}, u32[]{:S(2)}) collective-permute-start(bf16[512,128]{1,0:T(8,128)(2,1)S(1)} %shard_map.69.cot_ref), channel_id=1, source_target_pairs={{0,1},{1,0},{2,3},{3,2},{4,5},{5,4},{6,7},{7,6},{8,9},{9,8},{10,11... | collective-permute-start | bytes 393224 | tf_op jit(solution)/shard_map/ppermute | solution.py:340
  13.3 7.7 %collective-permute-start.3 = (bf16[512,128]{1,0:T(8,128)(2,1)S(1)}, bf16[512,128]{1,0:T(8,128)(2,1)S(1)}, u32[]{:S(2)}, u32[]{:S(2)}) collective-permute-start(bf16[512,128]{1,0:T(8,128)(2,1)S(1)} %get-tuple-element.35.refs_1_), channel_id=1, source_target_pairs={{0,3},{1,2},{2,1},{3,0},{4,7},{5,6},{6,5},{7,4},{8,11},{9,10},{10,... | collective-permute-start | bytes 393224 | tf_op jit(solution)/shard_map/ppermute | solution.py:340
  18.4 7.1 %collective-permute-start.6 = (bf16[2,64,512]{2,1,0:T(8,128)(2,1)S(1)}, bf16[2,64,512]{2,1,0:T(8,128)(2,1)S(1)}, u32[]{:S(2)}, u32[]{:S(2)}) collective-permute-start(bf16[2,64,512]{2,1,0:T(8,128)(2,1)S(1)} %get-tuple-element.37), channel_id=1, source_target_pairs={{0,1},{1,0},{2,3},{3,2},{4,5},{5,4},{6,7},{7,6},{8,9},{9,8},{10,11... | collective-permute-start | bytes 393224 | tf_op jit(solution)/shard_map/ppermute | solution.py:340
  19.7 11.5 %collective-permute-start.4 = (bf16[256,128]{1,0:T(8,128)(2,1)S(1)}, bf16[256,128]{1,0:T(8,128)(2,1)S(1)}, u32[]{:S(2)}, u32[]{:S(2)}) collective-permute-start(bf16[256,128]{1,0:T(8,128)(2,1)S(1)} %shard_map.71), channel_id=1, source_target_pairs={{0,3},{1,2},{2,1},{3,0},{4,7},{5,6},{6,5},{7,4},{8,11},{9,10},{10,... | collective-permute-start | bytes 196616 | tf_op jit(solution)/shard_map/ppermute | solution.py:340
  21.1 10.1 %collective-permute-start.5 = (bf16[256,128]{1,0:T(8,128)(2,1)S(1)}, bf16[256,128]{1,0:T(8,128)(2,1)S(1)}, u32[]{:S(2)}, u32[]{:S(2)}) collective-permute-start(bf16[256,128]{1,0:T(8,128)(2,1)S(1)} %shard_map.72), channel_id=1, source_target_pairs={{0,1},{1,0},{2,3},{3,2},{4,5},{5,4},{6,7},{7,6},{8,9},{9,8},{10,11... | collective-permute-start | bytes 196616 | tf_op jit(solution)/shard_map/ppermute | solution.py:340
  32.0 2.4 %collective-permute-start.7 = (bf16[2304,128]{1,0:T(8,128)(2,1)S(1)}, bf16[2304,128]{1,0:T(8,128)(2,1)S(1)}, u32[]{:S(2)}, u32[]{:S(2)}) collective-permute-start(bf16[2304,128]{1,0:T(8,128)(2,1)S(1)} %get-tuple-element.39), channel_id=1, source_target_pairs={{0,4},{4,0},{8,12},{12,8},{16,20},{20,16},{24,28},{28,24},{32,36},... | collective-permute-start | bytes 1769480 | tf_op jit(solution)/shard_map/ppermute | solution.py:395
  35.3 20.4 %all-to-all-start = ((bf16[32,37,2,128]{3,2,1,0:T(2,128)(2,1)}), bf16[32,37,2,128]{3,2,1,0:T(2,128)(2,1)S(1)}, u32[]{:S(2)}, u32[]{:S(2)}) async-start(bf16[32,37,2,128]{3,2,1,0:T(2,128)(2,1)} %bitcast.6), calls=%async_computation | async-start | bytes 1212416 | tf_op jit(solution)/shard_map/all_to_all | solution.py:409
  44.9 9.9 %collective-permute-start.8 = (bf16[64,512]{1,0:T(8,128)(2,1)S(1)}, bf16[64,512]{1,0:T(8,128)(2,1)S(1)}, u32[]{:S(2)}, u32[]{:S(2)}) collective-permute-start(bf16[64,512]{1,0:T(8,128)(2,1)S(1)} %get-tuple-element.44), channel_id=1, source_target_pairs={{0,3},{1,2},{2,1},{3,0},{4,7},{5,6},{6,5},{7,4},{8,11},{9,10},{10,... | collective-permute-start | bytes 196616 | tf_op jit(solution)/shard_map/ppermute | solution.py:340
  71.4 5.3 %collective-permute-start.9 = (bf16[2368,128]{1,0:T(8,128)(2,1)S(1)}, bf16[2368,128]{1,0:T(8,128)(2,1)S(1)}, u32[]{:S(2)}, u32[]{:S(2)}) collective-permute-start(bf16[2368,128]{1,0:T(8,128)(2,1)S(1)} %bitcast.15), channel_id=1, source_target_pairs={{0,4},{4,0},{8,12},{12,8},{16,20},{20,16},{24,28},{28,24},{32,36},... | collective-permute-start | bytes 1818632 | tf_op jit(solution)/shard_map/ppermute | solution.py:424

commit v4 on v3

--- a/solution.py
+++ b/solution.py
@@ -47,13 +47,13 @@
 
 
 def edges_kernel(
-    video_ref, own_ref, outer_ref, inner_ref, video_out, own_out, rows, pixels, packed
+    both_ref, outer_ref, inner_ref, video_out, own_out, rows, pixels, packed
 ):
     core = lax.axis_index("band") % 2
-    video_out[...] = video_ref[...]
-    own_out[...] = own_ref[...]
-    rows[...] = own_ref[...].astype(F32)
-    pixels[:48, :] = video_ref[...].astype(F32)
+    video_out[...] = both_ref[:48, 128:]
+    own_out[...] = both_ref[:, :128]
+    rows[...] = both_ref[:, :128].astype(F32)
+    pixels[:48, :] = both_ref[:48, 128:].astype(F32)
 
     def put(ref, r):
         ref[:128, :] = rows[pl.ds(r, 128, stride=2), :].astype(BF)
@@ -167,7 +167,7 @@
 
 def second_grad_kernel(
     xc_ref, c0_ref, c1_ref, c3_ref, own2_ref, outer2_ref, lkeep_ref, lgot_ref,
-    grown, keep_ref, send_ref, lown_ref, lsend_ref, rows, *, scale
+    grown, send_ref, lown_ref, lsend_ref, rows, *, scale
 ):
     lown_ref[...] = lkeep_ref[0].astype(F32) + lgot_ref[0].astype(F32)
     lsend_ref[...] = (lkeep_ref[1].astype(F32) + lgot_ref[1].astype(F32)).astype(BF)
@@ -190,21 +190,26 @@
                 part = rows[pl.ds(256 + side * 128 + f, 64, stride=2), :]
                 grown[pl.ds(at, 64), lane : lane + 128] = part.astype(BF)
 
-    def put(early_ref, late_ref):
-        c1 = grown[:, 640:896]
-        early = dot(xc_ref[:, :256], c1, 1, 1) * scale
-        late = (dot(xc_ref[:, :256], grown[:, 128:384], 1, 1) + dot(xc_ref[:, 256:], c1, 1, 1)) * scale
-        for ref, g in ((early_ref, early), (late_ref, late)):
-            ref[:1152, :] = g[:, :128].astype(BF)
-            ref[1152:, :] = g[:, 128:].astype(BF)
-
-    @pl.when(core == 0)
+    half_gradient(xc_ref, grown, send_ref, 1 - core, scale)
+
+
+def half_gradient(xc_ref, grown, out_ref, half, scale):
+    def put(g):
+        g = g * scale
+        out_ref[:1152, :] = g[:, :128].astype(BF)
+        out_ref[1152:, :] = g[:, 128:].astype(BF)
+
+    @pl.when(half == 0)
     def _():
-        put(keep_ref, send_ref)
-
-    @pl.when(core == 1)
+        put(dot(xc_ref[:, :256], grown[:, 640:896], 1, 1))
+
+    @pl.when(half == 1)
     def _():
-        put(send_ref, keep_ref)
+        put(dot(xc_ref[:, :256], grown[:, 128:384], 1, 1) + dot(xc_ref[:, 256:], grown[:, 640:896], 1, 1))
+
+
+def kept_kernel(xc_ref, grown, keep_ref, *, scale):
+    half_gradient(xc_ref, grown, keep_ref, lax.axis_index("band") % 2, scale)
 
 
 def backward_kernel(grown, pre_ref, win_ref, w2_ref, sel_ref, g1_ref, back_s, *, scale):
@@ -344,7 +349,7 @@
         [((272, 128), BF), ((272, 128), BF), ((48, 512), BF), ((256, 128), BF)],
         [((256, 128), F32), ((64, 512), F32), ((160, 128), F32)],
         1 << 20,
-        flat, own,
+        jnp.concatenate([own, jnp.pad(flat, ((0, 208), (0, 0)))], 1),
     )
     outer = lax.ppermute(outer, "band", [(i, i + 1 - 2 * (i % 2 == 0)) for i in range(1, n - 1)])
     inner = lax.ppermute(inner, "band", flip)
@@ -381,10 +386,10 @@
     def second_grad(*refs):
         second_grad_kernel(*refs, scale=scale_two)
 
-    cot, keep, send, lat_own, lat_send = call(
+    cot, send, lat_own, lat_send = call(
         second_grad,
         [
-            ((256, 1024), BF), ((2304, 128), BF), ((2304, 128), BF),
+            ((256, 1024), BF), ((2304, 128), BF),
             ((64, 512), F32), ((64, 512), BF),
         ],
         [((512, 128), F32)],
@@ -393,6 +398,11 @@
     )
     lat_got = swap(lat_send, 3)
     got = lax.ppermute(send, "band", flip)
+
+    def kept(*refs):
+        kept_kernel(*refs, scale=scale_two)
+
+    (keep,) = call(kept, [((2304, 128), BF)], [], 1 << 30, xc, cot)
 
     def backward(*refs):
         backward_kernel(*refs, scale=scale_one)

time: 78.2 us -> 77.8 us (level)
  local copies, waits for them, and re-layouts: 2.63 us -> 1 us
  other arithmetic: 0 us -> 1.02 us
    unnamed x7 -> x3, local copies, waits for them, and re-layouts: 1.65 us -> 0.02 us
    concatenate x0 -> x1, other arithmetic: none -> 1.02 us  [on_device(): jnp.concatenate([own, jnp.pad(flat, ((0, 208), (0, 0)))], 1)]
    pallas_call x13 -> x14, Pallas kernels: 9.16 us -> 9.39 us  [call(): pl.pallas_call(kernel, out_shape=[jax.ShapeDtypeStruct(*o) for o in outs]...]
  transfers between devices with their start and end apart: 11 -> 11, of which waited for: 8 -> 7; matrix products, arithmetic and copies ran while one was open for 1% -> 1% of each run, Pallas kernels for 7% -> 8%
where the time goes in v4:
time: 77.8 us; the launch traced here: 77.5 us
  starting transfers between devices  31.3 us (40%)
  waiting for transfers between devices  19.3 us (25%)
  blocking collectives  14.7 us (19%)
  Pallas kernels  9.39 us (12%)
  other arithmetic  1.02 us (1%)
  local copies, waits for them, and re-layouts  1 us (1%)
    ppermute x6, waiting for transfers between devices, swap(): return lax.ppermute(x, 'chan', [(i, i ^ k) for i in range(4)])  17.2 us
    all_to_all x1, blocking collectives, exchange(): x = lax.all_to_all(x, 'band', 0, 0, tiled=True, axis_index_groups=groups)  14.7 us
    ppermute x6, starting transfers between devices, swap(): return lax.ppermute(x, 'chan', [(i, i ^ k) for i in range(4)])  12.5 us
    all_to_all x1, starting transfers between devices, exchange(): x = lax.all_to_all(x, 'band', 0, 0, tiled=True, axis_index_groups=groups)  9.54 us
    pallas_call x14, Pallas kernels, call(): pl.pallas_call(kernel, out_shape=[jax.ShapeDtypeStruct(*o) for o in outs]...  9.39 us
    ppermute x1, starting transfers between devices, on_device(): lax.ppermute(outer, 'band', [(i, i + 1 - 2 * (i % 2 == 0)) for i in range...  4.6 us
    ppermute x1, starting transfers between devices, on_device(): other = lax.ppermute(mine, 'band', flip)  3.64 us
    all_to_all x1, waiting for transfers between devices, exchange(): x = lax.all_to_all(x, 'band', 0, 0, tiled=True, axis_index_groups=groups)  1.59 us
  transfers between devices with their start and end apart: 11, of which 7 were waited for; matrix products, arithmetic and copies ran while one was open for 1% of the time, Pallas kernels for 8%

profile of v4, /device:TPU:1, one launch (start us, length us, event | category | flops | bytes accessed | tf_op | source)
XLA Modules:
  0.0 77.5 jit_solution(15646461169002636961)
XLA Ops:
  0.6 1.0 %fusion.1.both_ref = bf16[256,640]{1,0:T(8,128)(2,1)S(1)} fusion(bf16[48,512]{1,0:T(8,128)(2,1)} %bitcast.24, bf16[256,128]{1,0:T(8,128)(2,1)} %bitcast.23), kind=kLoop, calls=%fused_computation.2 | loop fusion | flops 983040 | bytes 442368 | tf_op jit(solution)/shard_map/concatenate | solution.py:352
  1.7 0.1 shard_map.67
  1.7 4.6 %collective-permute-start = (bf16[272,128]{1,0:T(8,128)(2,1)S(1)}, bf16[272,128]{1,0:T(8,128)(2,1)S(1)}, u32[]{:S(2)}, u32[]{:S(2)}) collective-permute-start(bf16[272,128]{1,0:T(8,128)(2,1)S(1)} %get-tuple-element.26), channel_id=1, source_target_pairs={{4,8},{8,4},{12,16},{16,12},{20,24},{24,20},{28,32},{32,28},{36,40... | collective-permute-start | bytes 208904 | tf_op jit(solution)/shard_map/ppermute | solution.py:354
  6.3 0.1 collective-permute-start.1
  6.4 0.9 %slice.3 = bf16[18,12,32]{2,0,1:T(8,128)(2,1)S(1)} slice(bf16[27,12,32]{2,0,1:T(8,128)(2,1)} %param.5), slice={[9:27], [0:12], [0:32]} | slice | bytes 27648 | tf_op jit(solution)/shard_map/slice | solution.py:362
  7.5 0.5 shard_map.68
  8.0 0.3 collective-permute-done.outer_ref
  8.4 3.1 %collective-permute-start.2 = (bf16[512,128]{1,0:T(8,128)(2,1)S(1)}, bf16[512,128]{1,0:T(8,128)(2,1)S(1)}, u32[]{:S(2)}, u32[]{:S(2)}) collective-permute-start(bf16[512,128]{1,0:T(8,128)(2,1)S(1)} %shard_map.69.cot_ref), channel_id=1, source_target_pairs={{0,1},{1,0},{2,3},{3,2},{4,5},{5,4},{6,7},{7,6},{8,9},{9,8},{10,11... | collective-permute-start | bytes 393224 | tf_op jit(solution)/shard_map/ppermute | solution.py:345
  11.4 1.2 %shard_map.70 = (bf16[1152,512]{1,0:T(8,128)(2,1)S(1)}, f32[128,512]{1,0:T(8,128)S(1)}, bf16[256,512]{1,0:T(8,128)(2,1)S(1)}, bf16[512,128]{1,0:T(8,128)(2,1)S(1)}) custom-call(bf16[272,128]{1,0:T(8,128)(2,1)S(1)} %collective-permute-done.outer_ref, bf16[48,512]{1,0:T(8,128)(2,1)S(1)} %get-tuple-element.27.own_ref, ...), custom_call_target="tpu_custom_call" | custom-call | flops 1073741824 | bytes 1048576 | tf_op jit(solution)/shard_map/pallas_call | solution.py:323
  12.6 4.3 %collective-permute-start.3 = (bf16[512,128]{1,0:T(8,128)(2,1)S(1)}, bf16[512,128]{1,0:T(8,128)(2,1)S(1)}, u32[]{:S(2)}, u32[]{:S(2)}) collective-permute-start(bf16[512,128]{1,0:T(8,128)(2,1)S(1)} %get-tuple-element.34.refs_1_), channel_id=1, source_target_pairs={{0,3},{1,2},{2,1},{3,0},{4,7},{5,6},{6,5},{7,4},{8,11},{9,10},{10,... | collective-permute-start | bytes 393224 | tf_op jit(solution)/shard_map/ppermute | solution.py:345
  16.9 0.7 shard_map.73
  17.6 1.3 %collective-permute-start.6 = (bf16[2,64,512]{2,1,0:T(8,128)(2,1)S(1)}, bf16[2,64,512]{2,1,0:T(8,128)(2,1)S(1)}, u32[]{:S(2)}, u32[]{:S(2)}) collective-permute-start(bf16[2,64,512]{2,1,0:T(8,128)(2,1)S(1)} %get-tuple-element.36), channel_id=1, source_target_pairs={{0,1},{1,0},{2,3},{3,2},{4,5},{5,4},{6,7},{7,6},{8,9},{9,8},{10,11... | collective-permute-start | bytes 393224 | tf_op jit(solution)/shard_map/ppermute | solution.py:345
  18.9 1.3 %collective-permute-start.4 = (bf16[256,128]{1,0:T(8,128)(2,1)S(1)}, bf16[256,128]{1,0:T(8,128)(2,1)S(1)}, u32[]{:S(2)}, u32[]{:S(2)}) collective-permute-start(bf16[256,128]{1,0:T(8,128)(2,1)S(1)} %shard_map.71), channel_id=1, source_target_pairs={{0,3},{1,2},{2,1},{3,0},{4,7},{5,6},{6,5},{7,4},{8,11},{9,10},{10,... | collective-permute-start | bytes 196616 | tf_op jit(solution)/shard_map/ppermute | solution.py:345
  20.3 0.1 collective-permute-done.3.in_ref.refs_3_
  20.3 1.4 %collective-permute-start.5 = (bf16[256,128]{1,0:T(8,128)(2,1)S(1)}, bf16[256,128]{1,0:T(8,128)(2,1)S(1)}, u32[]{:S(2)}, u32[]{:S(2)}) collective-permute-start(bf16[256,128]{1,0:T(8,128)(2,1)S(1)} %shard_map.72), channel_id=1, source_target_pairs={{0,1},{1,0},{2,3},{3,2},{4,5},{5,4},{6,7},{7,6},{8,9},{9,8},{10,11... | collective-permute-start | bytes 196616 | tf_op jit(solution)/shard_map/ppermute | solution.py:345
  21.7 3.0 %collective-permute-done.6.refs_7_ = bf16[2,64,512]{2,1,0:T(8,128)(2,1)S(1)} collective-permute-done((bf16[2,64,512]{2,1,0:T(8,128)(2,1)S(1)}, bf16[2,64,512]{2,1,0:T(8,128)(2,1)S(1)}, u32[]{:S(2)}, u32[]{:S(2)}) %collective-permute-start.6) | collective-permute-done | bytes 131104 | tf_op jit(solution)/shard_map/ppermute | solution.py:345
  24.7 5.6 %collective-permute-done.4.refs_4_ = bf16[256,128]{1,0:T(8,128)(2,1)S(1)} collective-permute-done((bf16[256,128]{1,0:T(8,128)(2,1)S(1)}, bf16[256,128]{1,0:T(8,128)(2,1)S(1)}, u32[]{:S(2)}, u32[]{:S(2)}) %collective-permute-start.4) | collective-permute-done | bytes 65568 | tf_op jit(solution)/shard_map/ppermute | solution.py:345
  30.4 0.6 shard_map.74
  31.0 0.9 %collective-permute-start.7 = (bf16[2304,128]{1,0:T(8,128)(2,1)S(1)}, bf16[2304,128]{1,0:T(8,128)(2,1)S(1)}, u32[]{:S(2)}, u32[]{:S(2)}) collective-permute-start(bf16[2304,128]{1,0:T(8,128)(2,1)S(1)} %get-tuple-element.38), channel_id=1, source_target_pairs={{0,4},{4,0},{8,12},{12,8},{16,20},{20,16},{24,28},{28,24},{32,36},... | collective-permute-start | bytes 1769480 | tf_op jit(solution)/shard_map/ppermute | solution.py:400
  31.9 0.5 shard_map.75.keep_ref
  32.4 1.4 %shard_map.76.g1_ref = bf16[64,128]{1,0:T(8,128)(2,1)S(1)} custom-call(bf16[256,1024]{1,0:T(8,128)(2,1)S(1)} %get-tuple-element.37.refs_1_.refs_0_, f32[128,512]{1,0:T(8,128)S(1)} %get-tuple-element.39.refs_1_, bf16[256,512]{1,0:T(8,128)(2,1)S(1)} %get-tuple-element.40.refs_2_, bf16[3456,256]{1,0:T(8,128)(2,1)S(1)} %bitcast.19, ...), custom_call_target="tpu_custom_call" | custom-call | flops 1073741824 | bytes 1048576 | tf_op jit(solution)/shard_map/pallas_call | solution.py:323
  33.8 1.0 %shard_map.77 = bf16[2368,128]{1,0:T(8,128)(2,1)} custom-call(bf16[2304,128]{1,0:T(8,128)(2,1)S(1)} %shard_map.75.keep_ref, bf16[2304,128]{1,0:T(8,128)(2,1)S(1)} %collective-permute-done.7.got_ref, bf16[64,128]{1,0:T(8,128)(2,1)S(1)} %shard_map.76.g1_ref), custom_call_target="tpu_custom_call" | custom-call | flops 1048576 | bytes 1048576 | tf_op jit(solution)/shard_map/pallas_call | solution.py:323
  34.8 9.5 %all-to-all-start = ((bf16[32,37,2,128]{3,2,1,0:T(2,128)(2,1)}), bf16[32,37,2,128]{3,2,1,0:T(2,128)(2,1)S(1)}, u32[]{:S(2)}, u32[]{:S(2)}) async-start(bf16[32,37,2,128]{3,2,1,0:T(2,128)(2,1)} %bitcast.6), calls=%async_computation | async-start | bytes 1212416 | tf_op jit(solution)/shard_map/all_to_all | solution.py:419
  44.3 1.2 %collective-permute-start.8 = (bf16[64,512]{1,0:T(8,128)(2,1)S(1)}, bf16[64,512]{1,0:T(8,128)(2,1)S(1)}, u32[]{:S(2)}, u32[]{:S(2)}) collective-permute-start(bf16[64,512]{1,0:T(8,128)(2,1)S(1)} %get-tuple-element.42), channel_id=1, source_target_pairs={{0,3},{1,2},{2,1},{3,0},{4,7},{5,6},{6,5},{7,4},{8,11},{9,10},{10,... | collective-permute-start | bytes 196616 | tf_op jit(solution)/shard_map/ppermute | solution.py:345
  45.5 8.5 %collective-permute-done.8.refs_2_ = bf16[64,512]{1,0:T(8,128)(2,1)S(1)} collective-permute-done((bf16[64,512]{1,0:T(8,128)(2,1)S(1)}, bf16[64,512]{1,0:T(8,128)(2,1)S(1)}, u32[]{:S(2)}, u32[]{:S(2)}) %collective-permute-start.8) | collective-permute-done | bytes 65568 | tf_op jit(solution)/shard_map/ppermute | solution.py:345
  54.0 1.6 %all-to-all-done = bf16[32,37,2,128]{3,2,1,0:T(2,128)(2,1)S(1)} async-done(((bf16[32,37,2,128]{3,2,1,0:T(2,128)(2,1)}), bf16[32,37,2,128]{3,2,1,0:T(2,128)(2,1)S(1)}, u32[]{:S(2)}, u32[]{:S(2)}) %all-to-all-start) | async-done | bytes 606240 | tf_op jit(solution)/shard_map/all_to_all | solution.py:419
  55.6 0.7 shard_map.78
  56.3 14.7 %all_to_all.10 = bf16[32,37,2,128]{3,2,1,0:T(2,128)(2,1)S(1)} all-to-all(bf16[32,37,2,128]{3,2,1,0:T(2,128)(2,1)S(1)} %bitcast.17), channel_id=1, replica_groups={{0,8,16,24,32,40,48,56,64,72,80,88,96,104,112,120,128,136,144,152,160,1..., dimensions={0} | all-to-all | bytes 1212416 | tf_op jit(solution)/shard_map/all_to_all | solution.py:419
  70.9 3.6 %collective-permute-start.9 = (bf16[2368,128]{1,0:T(8,128)(2,1)S(1)}, bf16[2368,128]{1,0:T(8,128)(2,1)S(1)}, u32[]{:S(2)}, u32[]{:S(2)}) collective-permute-start(bf16[2368,128]{1,0:T(8,128)(2,1)S(1)} %bitcast.15), channel_id=1, source_target_pairs={{0,4},{4,0},{8,12},{12,8},{16,20},{20,16},{24,28},{28,24},{32,36},... | collective-permute-start | bytes 1818632 | tf_op jit(solution)/shard_map/ppermute | solution.py:434
  74.6 1.5 %shard_map.79 = (f32[3,1152,256]{2,1,0:T(8,128)}, bf16[64,128]{1,0:T(8,128)(2,1)S(1)}) custom-call(bf16[2368,128]{1,0:T(8,128)(2,1)S(1)} %bitcast.16), custom_call_target="tpu_custom_call" | custom-call | flops 1048576 | bytes 1048576 | tf_op jit(solution)/shard_map/pallas_call | solution.py:323
  76.1 0.1 collective-permute-done.9.other_ref
  76.2 1.2 %shard_map.80 = (f32[3,1152,256]{2,1,0:T(8,128)}, f32[12,27,32]{2,1,0:T(8,128)}) custom-call(f32[3,1152,256]{2,1,0:T(8,128)} %get-tuple-element.45._, bf16[64,128]{1,0:T(8,128)(2,1)S(1)} %get-tuple-element.46.mine_ref, bf16[2368,128]{1,0:T(8,128)(2,1)S(1)} %collective-permute-done.9.other_ref), custom_call_target="tpu_custom_call", output_to_operand_aliasing={{0}: (0, {})} | custom-call | flops 1048576 | bytes 1048576 | tf_op jit(solution)/shard_map/pallas_call | solution.py:323
  (13 shorter events, 0.1 us)
Async XLA Ops:
  0.6 16.3 %copy-start = (bf16[27,128,256]{2,1,0:T(8,128)(2,1)S(1)}, bf16[27,128,256]{2,1,0:T(8,128)(2,1)}, u32[]{:S(2)}) copy-start(bf16[27,128,256]{2,1,0:T(8,128)(2,1)} %param.6) | copy-start | bytes 5308420
  1.7 6.6 %collective-permute-start = (bf16[272,128]{1,0:T(8,128)(2,1)S(1)}, bf16[272,128]{1,0:T(8,128)(2,1)S(1)}, u32[]{:S(2)}, u32[]{:S(2)}) collective-permute-start(bf16[272,128]{1,0:T(8,128)(2,1)S(1)} %get-tuple-element.26), channel_id=1, source_target_pairs={{4,8},{8,4},{12,16},{16,12},{20,24},{24,20},{28,32},{32,28},{36,40... | collective-permute-start | bytes 208904 | tf_op jit(solution)/shard_map/ppermute | solution.py:354
  6.3 2.0 %collective-permute-start.1 = (bf16[272,128]{1,0:T(8,128)(2,1)S(1)}, bf16[272,128]{1,0:T(8,128)(2,1)S(1)}, u32[]{:S(2)}, u32[]{:S(2)}) collective-permute-start(bf16[272,128]{1,0:T(8,128)(2,1)S(1)} %get-tuple-element.28), channel_id=1, source_target_pairs={{0,4},{4,0},{8,12},{12,8},{16,20},{20,16},{24,28},{28,24},{32,36},... | collective-permute-start | bytes 208904 | tf_op jit(solution)/shard_map/ppermute | solution.py:355
  8.4 10.6 %collective-permute-start.2 = (bf16[512,128]{1,0:T(8,128)(2,1)S(1)}, bf16[512,128]{1,0:T(8,128)(2,1)S(1)}, u32[]{:S(2)}, u32[]{:S(2)}) collective-permute-start(bf16[512,128]{1,0:T(8,128)(2,1)S(1)} %shard_map.69.cot_ref), channel_id=1, source_target_pairs={{0,1},{1,0},{2,3},{3,2},{4,5},{5,4},{6,7},{7,6},{8,9},{9,8},{10,11... | collective-permute-start | bytes 393224 | tf_op jit(solution)/shard_map/ppermute | solution.py:345
  12.6 7.7 %collective-permute-start.3 = (bf16[512,128]{1,0:T(8,128)(2,1)S(1)}, bf16[512,128]{1,0:T(8,128)(2,1)S(1)}, u32[]{:S(2)}, u32[]{:S(2)}) collective-permute-start(bf16[512,128]{1,0:T(8,128)(2,1)S(1)} %get-tuple-element.34.refs_1_), channel_id=1, source_target_pairs={{0,3},{1,2},{2,1},{3,0},{4,7},{5,6},{6,5},{7,4},{8,11},{9,10},{10,... | collective-permute-start | bytes 393224 | tf_op jit(solution)/shard_map/ppermute | solution.py:345
  17.6 7.1 %collective-permute-start.6 = (bf16[2,64,512]{2,1,0:T(8,128)(2,1)S(1)}, bf16[2,64,512]{2,1,0:T(8,128)(2,1)S(1)}, u32[]{:S(2)}, u32[]{:S(2)}) collective-permute-start(bf16[2,64,512]{2,1,0:T(8,128)(2,1)S(1)} %get-tuple-element.36), channel_id=1, source_target_pairs={{0,1},{1,0},{2,3},{3,2},{4,5},{5,4},{6,7},{7,6},{8,9},{9,8},{10,11... | collective-permute-start | bytes 393224 | tf_op jit(solution)/shard_map/ppermute | solution.py:345
  18.9 11.4 %collective-permute-start.4 = (bf16[256,128]{1,0:T(8,128)(2,1)S(1)}, bf16[256,128]{1,0:T(8,128)(2,1)S(1)}, u32[]{:S(2)}, u32[]{:S(2)}) collective-permute-start(bf16[256,128]{1,0:T(8,128)(2,1)S(1)} %shard_map.71), channel_id=1, source_target_pairs={{0,3},{1,2},{2,1},{3,0},{4,7},{5,6},{6,5},{7,4},{8,11},{9,10},{10,... | collective-permute-start | bytes 196616 | tf_op jit(solution)/shard_map/ppermute | solution.py:345
  20.3 10.1 %collective-permute-start.5 = (bf16[256,128]{1,0:T(8,128)(2,1)S(1)}, bf16[256,128]{1,0:T(8,128)(2,1)S(1)}, u32[]{:S(2)}, u32[]{:S(2)}) collective-permute-start(bf16[256,128]{1,0:T(8,128)(2,1)S(1)} %shard_map.72), channel_id=1, source_target_pairs={{0,1},{1,0},{2,3},{3,2},{4,5},{5,4},{6,7},{7,6},{8,9},{9,8},{10,11... | collective-permute-start | bytes 196616 | tf_op jit(solution)/shard_map/ppermute | solution.py:345
  31.0 2.8 %collective-permute-start.7 = (bf16[2304,128]{1,0:T(8,128)(2,1)S(1)}, bf16[2304,128]{1,0:T(8,128)(2,1)S(1)}, u32[]{:S(2)}, u32[]{:S(2)}) collective-permute-start(bf16[2304,128]{1,0:T(8,128)(2,1)S(1)} %get-tuple-element.38), channel_id=1, source_target_pairs={{0,4},{4,0},{8,12},{12,8},{16,20},{20,16},{24,28},{28,24},{32,36},... | collective-permute-start | bytes 1769480 | tf_op jit(solution)/shard_map/ppermute | solution.py:400
  34.8 20.8 %all-to-all-start = ((bf16[32,37,2,128]{3,2,1,0:T(2,128)(2,1)}), bf16[32,37,2,128]{3,2,1,0:T(2,128)(2,1)S(1)}, u32[]{:S(2)}, u32[]{:S(2)}) async-start(bf16[32,37,2,128]{3,2,1,0:T(2,128)(2,1)} %bitcast.6), calls=%async_computation | async-start | bytes 1212416 | tf_op jit(solution)/shard_map/all_to_all | solution.py:419
  44.3 9.7 %collective-permute-start.8 = (bf16[64,512]{1,0:T(8,128)(2,1)S(1)}, bf16[64,512]{1,0:T(8,128)(2,1)S(1)}, u32[]{:S(2)}, u32[]{:S(2)}) collective-permute-start(bf16[64,512]{1,0:T(8,128)(2,1)S(1)} %get-tuple-element.42), channel_id=1, source_target_pairs={{0,3},{1,2},{2,1},{3,0},{4,7},{5,6},{6,5},{7,4},{8,11},{9,10},{10,... | collective-permute-start | bytes 196616 | tf_op jit(solution)/shard_map/ppermute | solution.py:345
  70.9 5.3 %collective-permute-start.9 = (bf16[2368,128]{1,0:T(8,128)(2,1)S(1)}, bf16[2368,128]{1,0:T(8,128)(2,1)S(1)}, u32[]{:S(2)}, u32[]{:S(2)}) collective-permute-start(bf16[2368,128]{1,0:T(8,128)(2,1)S(1)} %bitcast.15), channel_id=1, source_target_pairs={{0,4},{4,0},{8,12},{12,8},{16,20},{20,16},{24,28},{28,24},{32,36},... | collective-permute-start | bytes 1818632 | tf_op jit(solution)/shard_map/ppermute | solution.py:434

commit v5 on v4

--- a/solution.py
+++ b/solution.py
@@ -149,6 +149,10 @@
 
 def first_rows_kernel(in_ref, _, out_ref):
     out_ref[...] = in_ref[:256, :]
+
+
+def hold_kernel(_, __, ___):
+    pass
 
 
 def last_rows_kernel(in_ref, out_ref):
@@ -381,6 +385,10 @@
     lat_keep, lat_send = call(
         latent_kernel, [((2, 64, 512), BF)] * 2, [((256, 512), BF)], 1 << 30, xc, w2
     )
+    (lat_send,) = call(
+        hold_kernel, [((2, 64, 512), BF)], [], 1 << 10, lat_send, near_part,
+        far=(0, 1), far_out=(0,), aliases={0: 0},
+    )
     lat_got = swap(lat_send, 1)
 
     def second_grad(*refs):

time: 77.8 us -> 79.6 us (1.023)
  starting transfers between devices: 31.3 us -> 37 us
  waiting for transfers between devices: 19.3 us -> 14.4 us
  blocking collectives: 14.7 us -> 15.7 us
    ppermute x6, starting transfers between devices: 12.5 us -> 16.7 us  [swap(): return lax.ppermute(x, 'chan', [(i, i ^ k) for i in range(4)])]
    ppermute x6, waiting for transfers between devices: 17.2 us -> 13.9 us  [swap(): return lax.ppermute(x, 'chan', [(i, i ^ k) for i in range(4)])]
    all_to_all x1, waiting for transfers between devices: 1.59 us -> 0.01 us  [exchange(): x = lax.all_to_all(x, 'band', 0, 0, tiled=True, axis_index_groups=groups)]
    all_to_all x1, starting transfers between devices: 9.54 us -> 10.9 us  [exchange(): x = lax.all_to_all(x, 'band', 0, 0, tiled=True, axis_index_groups=groups)]
    all_to_all x1, blocking collectives: 14.7 us -> 15.7 us  [exchange(): x = lax.all_to_all(x, 'band', 0, 0, tiled=True, axis_index_groups=groups)]
    pallas_call x14 -> x15, Pallas kernels: 9.39 us -> 9.41 us  [call(): pl.pallas_call(kernel, out_shape=[jax.ShapeDtypeStruct(*o) for o in outs]...]
  transfers between devices with their start and end apart: 11 -> 11, of which waited for: 7 -> 5; matrix products, arithmetic and copies ran while one was open for 1% -> 1% of each run, Pallas kernels for 8% -> 7%
where the time goes in v5:
time: 79.6 us; the launch traced here: 79.3 us
  starting transfers between devices  37 us (46%)
  blocking collectives  15.7 us (20%)
  waiting for transfers between devices  14.4 us (18%)
  Pallas kernels  9.41 us (12%)
  other arithmetic  1.02 us (1%)
  local copies, waits for them, and re-layouts  1 us (1%)
  between operations  0.8 us (1%)
    ppermute x6, starting transfers between devices, swap(): return lax.ppermute(x, 'chan', [(i, i ^ k) for i in range(4)])  16.7 us
    all_to_all x1, blocking collectives, exchange(): x = lax.all_to_all(x, 'band', 0, 0, tiled=True, axis_index_groups=groups)  15.7 us
    ppermute x6, waiting for transfers between devices, swap(): return lax.ppermute(x, 'chan', [(i, i ^ k) for i in range(4)])  13.9 us
    all_to_all x1, starting transfers between devices, exchange(): x = lax.all_to_all(x, 'band', 0, 0, tiled=True, axis_index_groups=groups)  10.9 us
    pallas_call x15, Pallas kernels, call(): pl.pallas_call(kernel, out_shape=[jax.ShapeDtypeStruct(*o) for o in outs]...  9.41 us
    ppermute x1, starting transfers between devices, on_device(): lax.ppermute(outer, 'band', [(i, i + 1 - 2 * (i % 2 == 0)) for i in range...  4.6 us
    ppermute x1, starting transfers between devices, on_device(): other = lax.ppermute(mine, 'band', flip)  3.6 us
  transfers between devices with their start and end apart: 11, of which 5 were waited for; matrix products, arithmetic and copies ran while one was open for 1% of the time, Pallas kernels for 7%

profile of v5, /device:TPU:1, one launch (start us, length us, event | category | flops | bytes accessed | tf_op | source)
XLA Modules:
  0.0 79.3 jit_solution(8576538693834921750)
XLA Ops:
  0.6 1.0 %fusion.1.both_ref = bf16[256,640]{1,0:T(8,128)(2,1)S(1)} fusion(bf16[48,512]{1,0:T(8,128)(2,1)} %bitcast.24, bf16[256,128]{1,0:T(8,128)(2,1)} %bitcast.23), kind=kLoop, calls=%fused_computation.2 | loop fusion | flops 983040 | bytes 442368 | tf_op jit(solution)/shard_map/concatenate | solution.py:356
  1.7 0.1 shard_map.67
  1.7 4.6 %collective-permute-start = (bf16[272,128]{1,0:T(8,128)(2,1)S(1)}, bf16[272,128]{1,0:T(8,128)(2,1)S(1)}, u32[]{:S(2)}, u32[]{:S(2)}) collective-permute-start(bf16[272,128]{1,0:T(8,128)(2,1)S(1)} %get-tuple-element.26), channel_id=1, source_target_pairs={{4,8},{8,4},{12,16},{16,12},{20,24},{24,20},{28,32},{32,28},{36,40... | collective-permute-start | bytes 208904 | tf_op jit(solution)/shard_map/ppermute | solution.py:358
  6.3 0.1 collective-permute-start.1
  6.4 0.9 %slice.3 = bf16[18,12,32]{2,0,1:T(8,128)(2,1)S(1)} slice(bf16[27,12,32]{2,0,1:T(8,128)(2,1)} %param.5), slice={[9:27], [0:12], [0:32]} | slice | bytes 27648 | tf_op jit(solution)/shard_map/slice | solution.py:366
  7.5 0.5 shard_map.68
  8.0 0.3 collective-permute-done.outer_ref
  8.3 0.0 collective-permute-done.1.inner_ref
  8.4 3.1 %collective-permute-start.2 = (bf16[512,128]{1,0:T(8,128)(2,1)S(1)}, bf16[512,128]{1,0:T(8,128)(2,1)S(1)}, u32[]{:S(2)}, u32[]{:S(2)}) collective-permute-start(bf16[512,128]{1,0:T(8,128)(2,1)S(1)} %shard_map.69.cot_ref), channel_id=1, source_target_pairs={{0,1},{1,0},{2,3},{3,2},{4,5},{5,4},{6,7},{7,6},{8,9},{9,8},{10,11... | collective-permute-start | bytes 393224 | tf_op jit(solution)/shard_map/ppermute | solution.py:349
  11.4 1.2 %shard_map.70 = (bf16[1152,512]{1,0:T(8,128)(2,1)S(1)}, f32[128,512]{1,0:T(8,128)S(1)}, bf16[256,512]{1,0:T(8,128)(2,1)S(1)}, bf16[512,128]{1,0:T(8,128)(2,1)S(1)}) custom-call(bf16[272,128]{1,0:T(8,128)(2,1)S(1)} %collective-permute-done.outer_ref, bf16[48,512]{1,0:T(8,128)(2,1)S(1)} %get-tuple-element.27.own_ref, ...), custom_call_target="tpu_custom_call" | custom-call | flops 1073741824 | bytes 1048576 | tf_op jit(solution)/shard_map/pallas_call | solution.py:327
  12.6 4.3 %collective-permute-start.3 = (bf16[512,128]{1,0:T(8,128)(2,1)S(1)}, bf16[512,128]{1,0:T(8,128)(2,1)S(1)}, u32[]{:S(2)}, u32[]{:S(2)}) collective-permute-start(bf16[512,128]{1,0:T(8,128)(2,1)S(1)} %get-tuple-element.34.refs_1_), channel_id=1, source_target_pairs={{0,3},{1,2},{2,1},{3,0},{4,7},{5,6},{6,5},{7,4},{8,11},{9,10},{10,... | collective-permute-start | bytes 393224 | tf_op jit(solution)/shard_map/ppermute | solution.py:349
  16.9 0.7 shard_map.73
  17.7 1.3 %collective-permute-start.6 = (bf16[2,64,512]{2,1,0:T(8,128)(2,1)S(1)}, bf16[2,64,512]{2,1,0:T(8,128)(2,1)S(1)}, u32[]{:S(2)}, u32[]{:S(2)}) collective-permute-start(bf16[2,64,512]{2,1,0:T(8,128)(2,1)S(1)} %shard_map.74), channel_id=1, source_target_pairs={{0,1},{1,0},{2,3},{3,2},{4,5},{5,4},{6,7},{7,6},{8,9},{9,8},{10,11... | collective-permute-start | bytes 393224 | tf_op jit(solution)/shard_map/ppermute | solution.py:349
  19.0 2.5 %collective-permute-start.4 = (bf16[256,128]{1,0:T(8,128)(2,1)S(1)}, bf16[256,128]{1,0:T(8,128)(2,1)S(1)}, u32[]{:S(2)}, u32[]{:S(2)}) collective-permute-start(bf16[256,128]{1,0:T(8,128)(2,1)S(1)} %shard_map.71.__), channel_id=1, source_target_pairs={{0,3},{1,2},{2,1},{3,0},{4,7},{5,6},{6,5},{7,4},{8,11},{9,10},{10,... | collective-permute-start | bytes 196616 | tf_op jit(solution)/shard_map/ppermute | solution.py:349
  21.5 0.0 collective-permute-done.3.in_ref.refs_3_
  21.5 1.2 %collective-permute-start.5 = (bf16[256,128]{1,0:T(8,128)(2,1)S(1)}, bf16[256,128]{1,0:T(8,128)(2,1)S(1)}, u32[]{:S(2)}, u32[]{:S(2)}) collective-permute-start(bf16[256,128]{1,0:T(8,128)(2,1)S(1)} %shard_map.72), channel_id=1, source_target_pairs={{0,1},{1,0},{2,3},{3,2},{4,5},{5,4},{6,7},{7,6},{8,9},{9,8},{10,11... | collective-permute-start | bytes 196616 | tf_op jit(solution)/shard_map/ppermute | solution.py:349
  22.7 1.5 %collective-permute-done.4.refs_4_ = bf16[256,128]{1,0:T(8,128)(2,1)S(1)} collective-permute-done((bf16[256,128]{1,0:T(8,128)(2,1)S(1)}, bf16[256,128]{1,0:T(8,128)(2,1)S(1)}, u32[]{:S(2)}, u32[]{:S(2)}) %collective-permute-start.4) | collective-permute-done | bytes 65568 | tf_op jit(solution)/shard_map/ppermute | solution.py:349
  24.2 3.8 %collective-permute-done.5.refs_5_ = bf16[256,128]{1,0:T(8,128)(2,1)S(1)} collective-permute-done((bf16[256,128]{1,0:T(8,128)(2,1)S(1)}, bf16[256,128]{1,0:T(8,128)(2,1)S(1)}, u32[]{:S(2)}, u32[]{:S(2)}) %collective-permute-start.5) | collective-permute-done | bytes 65568 | tf_op jit(solution)/shard_map/ppermute | solution.py:349
  28.0 0.6 shard_map.75
  28.6 1.0 %collective-permute-start.7 = (bf16[2304,128]{1,0:T(8,128)(2,1)S(1)}, bf16[2304,128]{1,0:T(8,128)(2,1)S(1)}, u32[]{:S(2)}, u32[]{:S(2)}) collective-permute-start(bf16[2304,128]{1,0:T(8,128)(2,1)S(1)} %get-tuple-element.38), channel_id=1, source_target_pairs={{0,4},{4,0},{8,12},{12,8},{16,20},{20,16},{24,28},{28,24},{32,36},... | collective-permute-start | bytes 1769480 | tf_op jit(solution)/shard_map/ppermute | solution.py:408
  29.7 0.5 shard_map.76.keep_ref
  30.2 1.4 %shard_map.77.g1_ref = bf16[64,128]{1,0:T(8,128)(2,1)S(1)} custom-call(bf16[256,1024]{1,0:T(8,128)(2,1)S(1)} %get-tuple-element.37.refs_1_.refs_0_, f32[128,512]{1,0:T(8,128)S(1)} %get-tuple-element.39.refs_1_, bf16[256,512]{1,0:T(8,128)(2,1)S(1)} %get-tuple-element.40.refs_2_, bf16[3456,256]{1,0:T(8,128)(2,1)S(1)} %bitcast.19, ...), custom_call_target="tpu_custom_call" | custom-call | flops 1073741824 | bytes 1048576 | tf_op jit(solution)/shard_map/pallas_call | solution.py:327
  31.6 1.0 %shard_map.78 = bf16[2368,128]{1,0:T(8,128)(2,1)} custom-call(bf16[2304,128]{1,0:T(8,128)(2,1)S(1)} %shard_map.76.keep_ref, bf16[2304,128]{1,0:T(8,128)(2,1)S(1)} %collective-permute-done.7.got_ref, bf16[64,128]{1,0:T(8,128)(2,1)S(1)} %shard_map.77.g1_ref), custom_call_target="tpu_custom_call" | custom-call | flops 1048576 | bytes 1048576 | tf_op jit(solution)/shard_map/pallas_call | solution.py:327
  32.6 10.9 %all-to-all-start = ((bf16[32,37,2,128]{3,2,1,0:T(2,128)(2,1)}), bf16[32,37,2,128]{3,2,1,0:T(2,128)(2,1)S(1)}, u32[]{:S(2)}, u32[]{:S(2)}) async-start(bf16[32,37,2,128]{3,2,1,0:T(2,128)(2,1)} %bitcast.6), calls=%async_computation | async-start | bytes 1212416 | tf_op jit(solution)/shard_map/all_to_all | solution.py:427
  43.5 4.3 %collective-permute-start.8 = (bf16[64,512]{1,0:T(8,128)(2,1)S(1)}, bf16[64,512]{1,0:T(8,128)(2,1)S(1)}, u32[]{:S(2)}, u32[]{:S(2)}) collective-permute-start(bf16[64,512]{1,0:T(8,128)(2,1)S(1)} %get-tuple-element.42), channel_id=1, source_target_pairs={{0,3},{1,2},{2,1},{3,0},{4,7},{5,6},{6,5},{7,4},{8,11},{9,10},{10,... | collective-permute-start | bytes 196616 | tf_op jit(solution)/shard_map/ppermute | solution.py:349
  47.8 8.6 %collective-permute-done.8.refs_2_ = bf16[64,512]{1,0:T(8,128)(2,1)S(1)} collective-permute-done((bf16[64,512]{1,0:T(8,128)(2,1)S(1)}, bf16[64,512]{1,0:T(8,128)(2,1)S(1)}, u32[]{:S(2)}, u32[]{:S(2)}) %collective-permute-start.8) | collective-permute-done | bytes 65568 | tf_op jit(solution)/shard_map/ppermute | solution.py:349
  56.4 0.7 shard_map.79
  57.1 15.7 %all_to_all.10 = bf16[32,37,2,128]{3,2,1,0:T(2,128)(2,1)S(1)} all-to-all(bf16[32,37,2,128]{3,2,1,0:T(2,128)(2,1)S(1)} %bitcast.17), channel_id=1, replica_groups={{0,8,16,24,32,40,48,56,64,72,80,88,96,104,112,120,128,136,144,152,160,1..., dimensions={0} | all-to-all | bytes 1212416 | tf_op jit(solution)/shard_map/all_to_all | solution.py:427
  72.8 3.6 %collective-permute-start.9 = (bf16[2368,128]{1,0:T(8,128)(2,1)S(1)}, bf16[2368,128]{1,0:T(8,128)(2,1)S(1)}, u32[]{:S(2)}, u32[]{:S(2)}) collective-permute-start(bf16[2368,128]{1,0:T(8,128)(2,1)S(1)} %bitcast.15), channel_id=1, source_target_pairs={{0,4},{4,0},{8,12},{12,8},{16,20},{20,16},{24,28},{28,24},{32,36},... | collective-permute-start | bytes 1818632 | tf_op jit(solution)/shard_map/ppermute | solution.py:442
  76.4 1.5 %shard_map.80 = (f32[3,1152,256]{2,1,0:T(8,128)}, bf16[64,128]{1,0:T(8,128)(2,1)S(1)}) custom-call(bf16[2368,128]{1,0:T(8,128)(2,1)S(1)} %bitcast.16), custom_call_target="tpu_custom_call" | custom-call | flops 1048576 | bytes 1048576 | tf_op jit(solution)/shard_map/pallas_call | solution.py:327
  77.9 0.1 collective-permute-done.9.other_ref
  78.1 1.2 %shard_map.81 = (f32[3,1152,256]{2,1,0:T(8,128)}, f32[12,27,32]{2,1,0:T(8,128)}) custom-call(f32[3,1152,256]{2,1,0:T(8,128)} %get-tuple-element.45._, bf16[64,128]{1,0:T(8,128)(2,1)S(1)} %get-tuple-element.46.mine_ref, bf16[2368,128]{1,0:T(8,128)(2,1)S(1)} %collective-permute-done.9.other_ref), custom_call_target="tpu_custom_call", output_to_operand_aliasing={{0}: (0, {})} | custom-call | flops 1048576 | bytes 1048576 | tf_op jit(solution)/shard_map/pallas_call | solution.py:327
  (14 shorter events, 0.1 us)
Async XLA Ops:
  0.6 16.3 %copy-start = (bf16[27,128,256]{2,1,0:T(8,128)(2,1)S(1)}, bf16[27,128,256]{2,1,0:T(8,128)(2,1)}, u32[]{:S(2)}) copy-start(bf16[27,128,256]{2,1,0:T(8,128)(2,1)} %param.6) | copy-start | bytes 5308420
  1.7 6.6 %collective-permute-start = (bf16[272,128]{1,0:T(8,128)(2,1)S(1)}, bf16[272,128]{1,0:T(8,128)(2,1)S(1)}, u32[]{:S(2)}, u32[]{:S(2)}) collective-permute-start(bf16[272,128]{1,0:T(8,128)(2,1)S(1)} %get-tuple-element.26), channel_id=1, source_target_pairs={{4,8},{8,4},{12,16},{16,12},{20,24},{24,20},{28,32},{32,28},{36,40... | collective-permute-start | bytes 208904 | tf_op jit(solution)/shard_map/ppermute | solution.py:358
  6.3 2.0 %collective-permute-start.1 = (bf16[272,128]{1,0:T(8,128)(2,1)S(1)}, bf16[272,128]{1,0:T(8,128)(2,1)S(1)}, u32[]{:S(2)}, u32[]{:S(2)}) collective-permute-start(bf16[272,128]{1,0:T(8,128)(2,1)S(1)} %get-tuple-element.28), channel_id=1, source_target_pairs={{0,4},{4,0},{8,12},{12,8},{16,20},{20,16},{24,28},{28,24},{32,36},... | collective-permute-start | bytes 208904 | tf_op jit(solution)/shard_map/ppermute | solution.py:359
  8.4 9.3 %collective-permute-start.2 = (bf16[512,128]{1,0:T(8,128)(2,1)S(1)}, bf16[512,128]{1,0:T(8,128)(2,1)S(1)}, u32[]{:S(2)}, u32[]{:S(2)}) collective-permute-start(bf16[512,128]{1,0:T(8,128)(2,1)S(1)} %shard_map.69.cot_ref), channel_id=1, source_target_pairs={{0,1},{1,0},{2,3},{3,2},{4,5},{5,4},{6,7},{7,6},{8,9},{9,8},{10,11... | collective-permute-start | bytes 393224 | tf_op jit(solution)/shard_map/ppermute | solution.py:349
  12.6 8.9 %collective-permute-start.3 = (bf16[512,128]{1,0:T(8,128)(2,1)S(1)}, bf16[512,128]{1,0:T(8,128)(2,1)S(1)}, u32[]{:S(2)}, u32[]{:S(2)}) collective-permute-start(bf16[512,128]{1,0:T(8,128)(2,1)S(1)} %get-tuple-element.34.refs_1_), channel_id=1, source_target_pairs={{0,3},{1,2},{2,1},{3,0},{4,7},{5,6},{6,5},{7,4},{8,11},{9,10},{10,... | collective-permute-start | bytes 393224 | tf_op jit(solution)/shard_map/ppermute | solution.py:349
  17.7 10.4 %collective-permute-start.6 = (bf16[2,64,512]{2,1,0:T(8,128)(2,1)S(1)}, bf16[2,64,512]{2,1,0:T(8,128)(2,1)S(1)}, u32[]{:S(2)}, u32[]{:S(2)}) collective-permute-start(bf16[2,64,512]{2,1,0:T(8,128)(2,1)S(1)} %shard_map.74), channel_id=1, source_target_pairs={{0,1},{1,0},{2,3},{3,2},{4,5},{5,4},{6,7},{7,6},{8,9},{9,8},{10,11... | collective-permute-start | bytes 393224 | tf_op jit(solution)/shard_map/ppermute | solution.py:349
  19.0 5.2 %collective-permute-start.4 = (bf16[256,128]{1,0:T(8,128)(2,1)S(1)}, bf16[256,128]{1,0:T(8,128)(2,1)S(1)}, u32[]{:S(2)}, u32[]{:S(2)}) collective-permute-start(bf16[256,128]{1,0:T(8,128)(2,1)S(1)} %shard_map.71.__), channel_id=1, source_target_pairs={{0,3},{1,2},{2,1},{3,0},{4,7},{5,6},{6,5},{7,4},{8,11},{9,10},{10,... | collective-permute-start | bytes 196616 | tf_op jit(solution)/shard_map/ppermute | solution.py:349
  21.5 6.6 %collective-permute-start.5 = (bf16[256,128]{1,0:T(8,128)(2,1)S(1)}, bf16[256,128]{1,0:T(8,128)(2,1)S(1)}, u32[]{:S(2)}, u32[]{:S(2)}) collective-permute-start(bf16[256,128]{1,0:T(8,128)(2,1)S(1)} %shard_map.72), channel_id=1, source_target_pairs={{0,1},{1,0},{2,3},{3,2},{4,5},{5,4},{6,7},{7,6},{8,9},{9,8},{10,11... | collective-permute-start | bytes 196616 | tf_op jit(solution)/shard_map/ppermute | solution.py:349
  28.6 3.0 %collective-permute-start.7 = (bf16[2304,128]{1,0:T(8,128)(2,1)S(1)}, bf16[2304,128]{1,0:T(8,128)(2,1)S(1)}, u32[]{:S(2)}, u32[]{:S(2)}) collective-permute-start(bf16[2304,128]{1,0:T(8,128)(2,1)S(1)} %get-tuple-element.38), channel_id=1, source_target_pairs={{0,4},{4,0},{8,12},{12,8},{16,20},{20,16},{24,28},{28,24},{32,36},... | collective-permute-start | bytes 1769480 | tf_op jit(solution)/shard_map/ppermute | solution.py:408
  32.6 23.9 %all-to-all-start = ((bf16[32,37,2,128]{3,2,1,0:T(2,128)(2,1)}), bf16[32,37,2,128]{3,2,1,0:T(2,128)(2,1)S(1)}, u32[]{:S(2)}, u32[]{:S(2)}) async-start(bf16[32,37,2,128]{3,2,1,0:T(2,128)(2,1)} %bitcast.6), calls=%async_computation | async-start | bytes 1212416 | tf_op jit(solution)/shard_map/all_to_all | solution.py:427
  43.5 12.9 %collective-permute-start.8 = (bf16[64,512]{1,0:T(8,128)(2,1)S(1)}, bf16[64,512]{1,0:T(8,128)(2,1)S(1)}, u32[]{:S(2)}, u32[]{:S(2)}) collective-permute-start(bf16[64,512]{1,0:T(8,128)(2,1)S(1)} %get-tuple-element.42), channel_id=1, source_target_pairs={{0,3},{1,2},{2,1},{3,0},{4,7},{5,6},{6,5},{7,4},{8,11},{9,10},{10,... | collective-permute-start | bytes 196616 | tf_op jit(solution)/shard_map/ppermute | solution.py:349
  72.8 5.3 %collective-permute-start.9 = (bf16[2368,128]{1,0:T(8,128)(2,1)S(1)}, bf16[2368,128]{1,0:T(8,128)(2,1)S(1)}, u32[]{:S(2)}, u32[]{:S(2)}) collective-permute-start(bf16[2368,128]{1,0:T(8,128)(2,1)S(1)} %bitcast.15), channel_id=1, source_target_pairs={{0,4},{4,0},{8,12},{12,8},{16,20},{20,16},{24,28},{28,24},{32,36},... | collective-permute-start | bytes 1818632 | tf_op jit(solution)/shard_map/ppermute | solution.py:442
